TPU v7x, 256 devices: a whole 4x4x8 slice. The times are simulated.
256 devices in a mesh: row: 64 (over y, z, core), col: 4 (over x).
Axes of the slice: x: 4, y: 4, z: 8, core: 2. Of those that a mesh axis runs over, the one named last changes fastest.
Arguments:
- entity_feats: bfloat16 [65536, 256], P(('col', 'row')), may hold values from -6 to 6
- class_map: int32 [65536], P(('col', 'row')), may hold values from 0 to 127, as said below
- tile_values: bfloat16 [8192, 128, 128], P(('row', 'col')), may hold values from -0.09375 to 0.09375
- tile_rows: int32 [8192], P(('row', 'col')), may hold values from 0 to 3
- tile_column_index: int32 [8192], P(('row', 'col')), may hold values from 0 to 63
- tile_rels: int32 [8192], P(('row', 'col')), may hold values from 0 to 499
- tile_counts: int32 [256], P(('row', 'col')), may hold values from 4 to 32, as said below
- coefficients: bfloat16 [500, 8], replicated, may hold values from -2 to 2
- bases: bfloat16 [8, 256, 256], replicated, may hold values from -0.375 to 0.375
- cotangent: bfloat16 [32768, 256], P(('row', 'col')), may hold values from -6 to 6
Outputs:
- layer_out: bfloat16 [32768, 256], P(('row', 'col'))
- grad_entities: float32 [65536, 256], P(('col', 'row'))
- grad_bases: float32 [8, 256, 256], replicated
- grad_coef: float32 [500, 8], replicated
Inputs may be any that keep to these rules, and one draw needn't show every extreme that they name: `class_map`: within every block of 256 entities, every class number 0 to 127 occurs at least once. `tile_counts`: tile slots of a device from its count onward are unused; some device has all 32 slots live in every draw.
All inputs are finite; a program needn't handle non-finite values.
Results may differ from a plain program's by a relative error of at most 0.006.
Values may be sent and summed in bfloat16 or wider, within the bound.
No kernel may reach another device: no remote copies, remote signals or barrier semaphores. Data moves between devices by JAX's collectives and lax.ppermute only.
A program may use at most 128 MiB of HBM per device.

v0:
```python
import jax
import jax.numpy as jnp
from jax import lax
from jax.sharding import PartitionSpec as P

TBLK = 32


def tile_weights(rel_block, row_block, live, coefficients, trows, relations):
    pick_rel = (rel_block[:, None] == jnp.arange(relations, dtype=jnp.int32)[None, :]).astype(
        jnp.bfloat16
    )
    coef_rows = jnp.dot(pick_rel, coefficients, preferred_element_type=jnp.float32)
    pick_row = (
        (row_block[:, None] == jnp.arange(trows, dtype=jnp.int32)[None, :]) & live[:, None]
    ).astype(jnp.float32)
    weights = (pick_row[:, :, None] * coef_rows[:, None, :]).astype(jnp.bfloat16)
    return (weights, pick_row)


def local(
    entity_feats,
    class_map,
    tile_values,
    tile_rows,
    tile_column_index,
    tile_rels,
    tile_counts,
    coefficients,
    bases,
    cotangent,
):
    n_row = lax.axis_size("row")
    n_col = lax.axis_size("col")
    node_dev = cotangent.shape[0]
    tile = tile_values.shape[1]
    nbases = bases.shape[0]
    width = bases.shape[1]
    relations = coefficients.shape[0]
    rblock = node_dev * n_col
    cblock = node_dev * n_row
    trows = rblock // tile
    tile_column_list = cblock // tile
    member = class_map[:, None] == jnp.arange(node_dev, dtype=jnp.int32)[None, :]
    member_bf = member.astype(jnp.bfloat16)
    sums = lax.dot_general(
        member_bf, entity_feats, (((0,), (0,)), ((), ())), preferred_element_type=jnp.float32
    )
    counts = jnp.sum(member.astype(jnp.float32), axis=0)
    class_feat = (sums / counts[:, None]).astype(jnp.bfloat16)
    sender_device = lax.all_gather(class_feat, "row", axis=0, tiled=True).reshape(
        tile_column_list, tile, width
    )
    stacked = bases.reshape(nbases * width, width)
    live_count = tile_counts[0]
    turns = (live_count + TBLK - 1) // TBLK

    def forward_turn(step, carry):
        sums_acc, msg_store = carry
        leading_entry = step * TBLK
        live = leading_entry + jnp.arange(TBLK, dtype=jnp.int32) < live_count
        selected_entries = jnp.take(sender_device, tile_column_index, axis=0)
        messages = jnp.einsum(
            "kij,kjh->kih", tile_values, selected_entries, preferred_element_type=jnp.float32
        ).astype(jnp.bfloat16)
        weights, pick_row = tile_weights(tile_rels, tile_rows, live, coefficients, trows, relations)
        sums_acc = sums_acc + jnp.einsum(
            "ktb,kih->tibh", weights, messages, preferred_element_type=jnp.float32
        )
        msg_store = messages
        return (sums_acc, msg_store)

    init_sums = jnp.zeros((trows, tile, nbases, width), jnp.float32)
    init_store = jnp.zeros((tile_values.shape[0], tile, width), jnp.bfloat16)
    sums_acc, msg_store = lax.fori_loop(0, turns, forward_turn, (init_sums, init_store))
    part = sums_acc.astype(jnp.bfloat16).reshape(rblock, nbases * width)
    out_part = jnp.dot(part, stacked, preferred_element_type=jnp.float32)
    layer_out = lax.psum_scatter(out_part, "col", scatter_dimension=0, tiled=True).astype(
        jnp.bfloat16
    )
    dout_rows = lax.all_gather(cotangent, "col", axis=0, tiled=True)
    grads_rows = lax.dot_general(
        dout_rows, stacked, (((1,), (1,)), ((), ())), preferred_element_type=jnp.float32
    ).astype(jnp.bfloat16)
    dv_part = lax.dot_general(
        part, dout_rows, (((0,), (0,)), ((), ())), preferred_element_type=jnp.float32
    )
    grads_tiles = grads_rows.reshape(trows, tile, nbases, width)

    def backward_turn(step, carry):
        dcoef_acc, dx_acc = carry
        leading_entry = step * TBLK
        live = leading_entry + jnp.arange(TBLK, dtype=jnp.int32) < live_count
        weights, pick_row = tile_weights(tile_rels, tile_rows, live, coefficients, trows, relations)
        gram = jnp.einsum(
            "kih,tibh->ktb", msg_store, grads_tiles, preferred_element_type=jnp.float32
        )
        per_tile = jnp.sum(gram * pick_row[:, :, None], axis=1)
        dcoef_acc = dcoef_acc + jax.ops.segment_sum(per_tile, tile_rels, num_segments=relations)
        mixed = jnp.einsum(
            "ktb,tibh->kih", weights, grads_tiles, preferred_element_type=jnp.float32
        ).astype(jnp.bfloat16)
        back = jnp.einsum("kij,kih->kjh", tile_values, mixed, preferred_element_type=jnp.float32)
        dx_acc = dx_acc.at[tile_column_index].add(back)
        return (dcoef_acc, dx_acc)

    init_coef = jnp.zeros((relations, nbases), jnp.float32)
    init_dx = jnp.zeros((tile_column_list, tile, width), jnp.float32)
    dcoef_acc, dx_acc = lax.fori_loop(0, turns, backward_turn, (init_coef, init_dx))
    dx_all = dx_acc.reshape(cblock, width)
    dx_own = lax.psum_scatter(dx_all, "row", scatter_dimension=0, tiled=True)
    dv_sum, dcoef_sum = lax.psum((dv_part, dcoef_acc), ("row", "col"))
    scale = (node_dev * n_row * n_col) ** (-0.5)
    grad_bases = (dv_sum * scale).reshape(nbases, width, width)
    grad_coef = dcoef_sum * scale
    quotient = dx_own / counts[:, None]
    grad_entities = jnp.dot(member.astype(jnp.float32), quotient, precision=lax.Precision.HIGHEST)
    return (layer_out, grad_entities, grad_bases, grad_coef)


def solution(mesh):
    placed = (
        P(("col", "row"), None),
        P(("col", "row")),
        P(("row", "col"), None, None),
        P(("row", "col")),
        P(("row", "col")),
        P(("row", "col")),
        P(("row", "col")),
        P(),
        P(),
        P(("row", "col"), None),
    )
    return jax.shard_map(
        local,
        mesh=mesh,
        in_specs=placed,
        out_specs=(P(("row", "col"), None), P(("col", "row"), None), P(), P()),
        check_vma=False,
    )
```

profile of v0, /device:TPU:1, one launch (start us, length us, event | category | flops | bytes accessed | tf_op | source)
XLA Modules:
  0.0 565.6 jit_solution(12668102719578885372)
XLA Ops:
  8.1 1.8 fusion.22
  10.7 11.2 %all_gather.7 = bf16[512,256]{1,0:T(8,128)(2,1)S(1)} all-gather(bf16[128,256]{1,0:T(8,128)(2,1)} %param.23), channel_id=1, replica_groups=mesh['row'=64,'col'=4] {'col'}, dimensions={0}, use_global_device_ids=true | all-gather | bytes 327680 | tf_op jit(solution)/shard_map/all_gather | solution.py:81
  23.2 0.9 fusion.32
  24.1 70.5 %all-gather.2.cloned.1.call-done = bf16[8192,256]{1,0:T(8,128)(2,1)} async-done(((bf16[128,256]{1,0:T(8,128)(2,1)}), bf16[8192,256]{1,0:T(8,128)(2,1)}) %all-gather.2.cloned.1.call-update) | async-done | bytes 4194320 | tf_op jit(solution)/shard_map/all_gather | solution.py:51
  94.7 4.3 gather_fusion
  99.0 3.8 convert_bitcast_fusion
  102.7 3.4 copy.35
  106.1 1.6 broadcast_in_dim.33
  107.7 2.3 broadcast_in_dim.32
  110.0 6.6 %while.31 = (s32[]{:T(128)}, f32[4,128,8,256]{3,2,1,0:T(8,128)}, bf16[32,128,256]{2,0,1:T(8,128)(2,1)}, s32[]{:T(128)}, s32[32]{0:T(128)S(1)}, /*index=5*/s32[]{...) while((s32[]{:T(128)}, f32[4,128,8,256]{3,2,1,0:T(8,128)}, ...), condition=%wide.region_2.3_spmd, body=%wide.region_1.2_spmd.sunk | while | flops 68159936 | bytes 48236912 | solution.py:75
  110.7 1.3 copy.62
  112.0 1.6 copy-done.1
  113.6 1.1 bitcast_add_fusion.2
  114.7 1.9 copy-done.2
  116.6 2.4 convert_element_type.73
  119.7 1.3 copy-done.5
  121.0 2.1 fusion.37
  124.9 1.3 copy-done.7
  126.9 0.9 copy-done.6
  127.8 1.5 fusion.36
  129.5 4.3 broadcast_in_dim.46
  133.7 22.3 %while.32 = (s32[]{:T(128)}, f32[500,8]{1,0:T(8,128)S(1)}, f32[64,128,256]{2,1,0:T(8,128)}, s32[]{:T(128)}, s32[32]{0:T(128)S(1)}, /*index=5*/s32[32]{0:T(128)S(...) while((s32[]{:T(128)}, f32[500,8]{1,0:T(8,128)S(1)}, ...), condition=%wide.region_8.9_spmd, body=%wide.region_4.8_spmd.sunk | while | flops 337646112 | bytes 36713844 | solution.py:109
  136.6 3.7 convolution_bitcast_fusion.2
  140.2 5.6 copy.51
  145.9 10.2 %scatter_fusion.1 = f32[64,128,256]{2,1,0:T(8,128)} fusion(f32[64,128,256]{2,1,0:T(8,128)} %get-tuple-element.645, s32[32]{0:T(128)S(1)} %fusion.66, f32[32,128,256]{2,1,0:T(8,128)} %copy.51), kind=kCustom, calls=%fused_computation.2.clone.1 | custom fusion | flops 1048576 | bytes 12583040 | tf_op jit(solution)/shard_map/while/body/scatter-add | solution.py:104
  156.2 75.5 %psum.15 = f32[500,8]{0,1:T(8,128)S(1)} all-reduce(f32[500,8]{0,1:T(8,128)S(1)} %copy.37), channel_id=1, replica_groups=mesh['row'=64,'col'=4] {'row','col'}, use_global_device_ids=true, to_apply=%region_11.12 | all-reduce | flops 4000 | bytes 32000 | tf_op jit(solution)/shard_map/psum | solution.py:112
  232.3 147.6 %all-reduce.2.cloned.1.call-done = f32[2048,256]{1,0:T(8,128)} async-done(((f32[2048,256]{1,0:T(8,128)}), f32[2048,256]{1,0:T(8,128)}) %all-reduce.2.cloned.1.call-update) | async-done | bytes 2097168 | tf_op jit(solution)/shard_map/psum | solution.py:112
  379.9 3.1 broadcast_multiply_fusion
  383.0 22.0 %reduce-scatter.3.cloned.1.call-done = f32[128,256]{1,0:T(8,128)} async-done(((f32[512,256]{1,0:T(8,128)}), f32[128,256]{1,0:T(8,128)}) %reduce-scatter.3.cloned.1.call-update) | async-done | bytes 131088 | tf_op jit(solution)/shard_map/reduce_scatter | solution.py:78
  405.0 1.5 convert_element_type.74
  406.5 150.6 %reduce-scatter.5.cloned.1.call-done = f32[128,256]{1,0:T(8,128)} async-done(((f32[8192,256]{1,0:T(8,128)}), f32[128,256]{1,0:T(8,128)}) %reduce-scatter.5.cloned.1.call-update) | async-done | bytes 131088 | tf_op jit(solution)/shard_map/reduce_scatter | solution.py:111
  557.1 2.0 fusion.27
  (48 shorter events, 9.7 us)
Async XLA Ops:
  7.2 116.0 %copy-start = (bf16[8,256,256]{2,1,0:T(8,128)(2,1)S(1)}, bf16[8,256,256]{2,1,0:T(8,128)(2,1)}, u32[]{:S(2)}) copy-start(bf16[8,256,256]{2,1,0:T(8,128)(2,1)} %param.22) | copy-start | bytes 3145732
  7.2 87.5 %all-gather.2.cloned.1.call-start = ((), (), s32[]{:S(2)}) async-start(), calls=%async_computation.2 | async-start | bytes 4259840 | tf_op jit(solution)/shard_map/all_gather | solution.py:51
  10.0 369.9 %all-reduce.2.cloned.1.call-start = ((), (), s32[]{:S(2)}) async-start(), calls=%async_computation.5 | async-start | bytes 4194304 | tf_op jit(solution)/shard_map/psum | solution.py:112
  94.7 4.3 copy-start.3
  107.7 2.3 copy-start.8
  110.7 2.9 copy-start.1
  114.7 1.9 copy-start.2
  119.7 1.3 copy-start.5
  123.1 281.8 %reduce-scatter.3.cloned.1.call-start = ((), (), s32[]{:S(2)}) async-start(), calls=%async_computation.3 | async-start | bytes 655360 | tf_op jit(solution)/shard_map/reduce_scatter | solution.py:78
  124.6 1.6 copy-start.7
  126.2 1.6 copy-start.6
  129.4 427.8 %reduce-scatter.5.cloned.1.call-start = ((), (), s32[]{:S(2)}) async-start(), calls=%async_computation.4 | async-start | bytes 8519680 | tf_op jit(solution)/shard_map/reduce_scatter | solution.py:111
  129.4 4.3 copy-start.9
  129.4 4.3 copy-start.11
  135.3 1.2 copy-start.4
  232.3 324.8 %copy-start.10 = (s32[256]{0:T(256)S(1)}, s32[256]{0:T(256)}, u32[]{:S(2)}) copy-start(s32[256]{0:T(256)} %param.15) | copy-start | bytes 3076
Sparse Core Ops, SparseCore 0:
  11.4 83.2 all-gather.1
  123.2 256.5 all-reduce.1
  382.4 22.5 reduce-scatter.2
  409.0 148.0 reduce-scatter.4
where the time goes:
time: 571 us; the launch traced here: 566 us
  waiting for transfers between devices  391 us (68%)
  blocking collectives  86.7 us (15%)
  local copies, waits for them, and re-layouts  32.2 us (6%)
  other arithmetic  22.2 us (4%)
  matrix products  18.9 us (3%)
  between operations  14.5 us (3%)
    reduce_scatter x1, waiting for transfers between devices, local(): dx_own = lax.psum_scatter(dx_all, 'row', scatter_dimension=0, tiled=True)  151 us
    psum x1, waiting for transfers between devices, local(): dv_sum, dcoef_sum = lax.psum((dv_part, dcoef_acc), ('row', 'col'))  148 us
    psum x1, blocking collectives, local(): dv_sum, dcoef_sum = lax.psum((dv_part, dcoef_acc), ('row', 'col'))  75.5 us
    all_gather x1, waiting for transfers between devices, local(): lax.all_gather(class_feat, 'row', axis=0, tiled=True)  70.5 us
    reduce_scatter x1, waiting for transfers between devices, local(): lax.psum_scatter(out_part, 'col', scatter_dimension=0, tiled=True)  22 us
  transfers between devices with their start and end apart: 4, of which 4 were waited for; matrix products, arithmetic and copies ran while one was open for 7% of the time, Pallas kernels for 0%

commit v1 on v0

v1 whole, which is shorter than its diff:
```python
import jax
import jax.numpy as jnp
from jax import lax
from jax.experimental import pallas as pl
from jax.experimental.pallas import tpu as pltpu
from jax.sharding import Mesh
from jax.sharding import PartitionSpec as P

NY, NZ, NC, NX = 4, 8, 2, 4
TILE = 128
H = 256
B = 8
SLOTS = 32
TROWS = 4
RELS = 500
F32, BF16 = jnp.float32, jnp.bfloat16
ROWS = ("y", "z", "c")
DEVICES = ("y", "z", "c", "x")
VMEM = pl.BlockSpec(memory_space=pltpu.VMEM)
SMEM = pl.BlockSpec(memory_space=pltpu.SMEM)
ANY = pl.BlockSpec(memory_space=pl.ANY)
PARAMS = pltpu.CompilerParams(vmem_limit_bytes=56 * 2**20)


def backward_kernel(
    trow, dslot, count, coef, cot, bases, tiles, grads, keep, give, total, mixed
):
    for t in range(TROWS):
        for b in range(B):
            g = lax.dot_general(
                cot[pl.ds(t * TILE, TILE), :],
                bases[pl.ds(b * H, H), :],
                (((1,), (1,)), ((), ())),
                preferred_element_type=F32,
            )
            grads[t, :, pl.ds(b * H, H)] = g.astype(BF16)
    total[...] = jnp.zeros_like(total)

    def turn(s, carry):
        t = trow[s]
        d = dslot[s]
        for r in range(4):
            rows = pl.ds(r * 32, 32)
            acc = coef[s, 0] * grads[t, rows, pl.ds(0, H)].astype(F32)
            for b in range(1, B):
                acc = acc + coef[s, b] * grads[t, rows, pl.ds(b * H, H)].astype(F32)
            mixed[rows, :] = acc.astype(BF16)
        back = lax.dot_general(
            tiles[s], mixed[...], (((0,), (0,)), ((), ())), preferred_element_type=F32
        )
        total[d] = total[d] + back
        return carry

    lax.fori_loop(0, count[0], turn, 0)
    keep[...] = total[pl.ds(0, SLOTS)]
    give[...] = total[pl.ds(SLOTS, SLOTS)].astype(BF16)


def backward(trow, dslot, count, coef, cot_rows, stacked, tile_values):
    blocks = (SLOTS, TILE, H)
    return pl.pallas_call(
        backward_kernel,
        in_specs=[SMEM, SMEM, SMEM, SMEM, VMEM, VMEM, VMEM],
        out_specs=[VMEM, VMEM, VMEM],
        out_shape=[
            jax.ShapeDtypeStruct((TROWS, TILE, B * H), BF16),
            jax.ShapeDtypeStruct(blocks, F32),
            jax.ShapeDtypeStruct(blocks, BF16),
        ],
        scratch_shapes=[
            pltpu.VMEM((2 * SLOTS, TILE, H), F32),
            pltpu.VMEM((TILE, H), BF16),
        ],
        compiler_params=PARAMS,
        name="backward",
    )(trow, dslot, count, coef, cot_rows, stacked, tile_values)


def forward_kernel(
    trow, xslot, count, half, coef, relc, relr, xmine, xother, tiles, grads, bases, cot,
    outp, dkeep, dgive, coefg,
    feats, sums, part, dv, msg, gram, sems,
):
    copies = [
        pltpu.make_async_copy(src, feats.at[pl.ds(k * SLOTS, SLOTS)], sems.at[k])
        for k, src in enumerate((xmine, xother))
    ]
    for copy in copies:
        copy.start()
    sums[...] = jnp.zeros_like(sums)
    gram[...] = jnp.zeros_like(gram)
    for copy in copies:
        copy.wait()

    def turn(s, carry):
        t = trow[s]
        m = jnp.dot(tiles[s], feats[xslot[s]], preferred_element_type=F32)
        msg[...] = m.astype(BF16).astype(F32)
        dots = [jnp.zeros((8, 128), F32) for _ in range(B)]
        for r in range(4):
            rows = pl.ds(r * 32, 32)
            mm = msg[rows, :]
            for b in range(B):
                cols = pl.ds(b * H, H)
                sums[t, rows, cols] = sums[t, rows, cols] + coef[s, b] * mm
                prod = mm * grads[t, rows, cols].astype(F32)
                fold = jnp.sum(prod.reshape(4, 8, H), axis=0)
                dots[b] = dots[b] + (fold[:, :128] + fold[:, 128:])
        for b in range(B):
            gram[s, b] = dots[b]
        return carry

    lax.fori_loop(0, count[0], turn, 0)

    for t in range(TROWS):
        part[t] = sums[t].astype(BF16)
        outp[t] = jnp.dot(part[t], bases[...], preferred_element_type=F32).astype(BF16)
    for b in range(B):
        acc = None
        for t in range(TROWS):
            d = lax.dot_general(
                part[t, :, pl.ds(b * H, H)],
                cot[pl.ds(t * TILE, TILE), :],
                (((0,), (0,)), ((), ())),
                preferred_element_type=F32,
            )
            acc = d if acc is None else acc + d
        dv[b // 4, pl.ds((b % 4) * H, H), :] = acc
    mine = half[0]
    dkeep[...] = dv[mine]
    dgive[pl.ds(0, 1024), :] = dv[1 - mine].astype(BF16)

    col = jnp.sum(jnp.sum(gram[...].reshape(SLOTS * B, 8, 128), axis=1), axis=1, keepdims=True)
    lane = lax.broadcasted_iota(jnp.int32, (SLOTS * B, 128), 1)
    row = lax.broadcasted_iota(jnp.int32, (SLOTS * B, 128), 0)
    pick = (lane % B == row % B) & (lane // B == relc[...] % 16)
    spread = jnp.where(pick, col, 0.0)
    line = lax.broadcasted_iota(jnp.int32, (32, SLOTS * B), 0)
    gather = (relr[...] // 16 == line).astype(F32)
    cg = jnp.dot(gather, spread, precision=lax.Precision.HIGHEST, preferred_element_type=F32)
    coefg[...] = cg
    hi = cg.astype(BF16)
    dgive[pl.ds(1024, 32), pl.ds(0, 128)] = hi
    dgive[pl.ds(1024, 32), pl.ds(128, 128)] = (cg - hi.astype(F32)).astype(BF16)


def forward(trow, xslot, count, half, coef, relc, relr, xmine, xother, tiles, grads, stacked, cot_rows):
    return pl.pallas_call(
        forward_kernel,
        in_specs=[SMEM] * 5 + [VMEM] * 2 + [ANY] * 2 + [VMEM] * 4,
        out_specs=[VMEM] * 4,
        out_shape=[
            jax.ShapeDtypeStruct((TROWS, TILE, H), BF16),
            jax.ShapeDtypeStruct((1024, H), F32),
            jax.ShapeDtypeStruct((1056, H), BF16),
            jax.ShapeDtypeStruct((32, 128), F32),
        ],
        scratch_shapes=[
            pltpu.VMEM((2 * SLOTS, TILE, H), BF16),
            pltpu.VMEM((TROWS, TILE, B * H), F32),
            pltpu.VMEM((TROWS, TILE, B * H), BF16),
            pltpu.VMEM((2, 1024, H), F32),
            pltpu.VMEM((TILE, H), F32),
            pltpu.VMEM((SLOTS, B, 8, 128), F32),
            pltpu.SemaphoreType.DMA((2,)),
        ],
        compiler_params=PARAMS,
        name="forward",
    )(trow, xslot, count, half, coef, relc, relr, xmine, xother, tiles, grads, stacked, cot_rows)


def swap(x):
    return lax.ppermute(x, "c", [(0, 1), (1, 0)])


def exchange(x, axes):
    return lax.all_to_all(x, axes, split_axis=0, concat_axis=0, tiled=True)


def spread_to(x, axes, n):
    return exchange(jnp.broadcast_to(x[None], (n,) + x.shape), axes)


def two_parts(x):
    hi = lax.reduce_precision(x, 8, 7)
    return jnp.concatenate([hi, x - hi], axis=-1).astype(BF16)


def after(x, y):
    return lax.optimization_barrier((x, y))


def local(
    entity_feats,
    class_map,
    tile_values,
    tile_rows,
    tile_column_index,
    tile_rels,
    tile_counts,
    coefficients,
    bases,
    cotangent,
):
    mine = lax.axis_index("c").astype(jnp.int32)
    member = class_map[:, None] == jnp.arange(TILE, dtype=jnp.int32)[None, :]
    sums = lax.dot_general(
        member.astype(BF16), entity_feats, (((0,), (0,)), ((), ())), preferred_element_type=F32
    )
    counts = jnp.sum(member.astype(F32), axis=0)
    class_feat = (sums / counts[:, None]).astype(BF16)

    pick_rel = (tile_rels[:, None] == jnp.arange(RELS, dtype=jnp.int32)[None, :]).astype(BF16)
    coef = jnp.dot(pick_rel, coefficients, preferred_element_type=F32)
    other = (tile_column_index % 2 != mine).astype(jnp.int32) * SLOTS
    ty = tile_column_index // (2 * NZ)
    tz = (tile_column_index // 2) % NZ
    xslot = other + ty * NZ + tz
    dslot = other + tz * NY + ty
    stacked = bases.reshape(B * H, H)

    with jax.named_scope("feats_z"):
        feats_z = spread_to(class_feat, "z", NZ).reshape(NZ * TILE, H)
    cotangent, feats_z = after(cotangent, feats_z)
    with jax.named_scope("feats_y"):
        feats_mine = lax.all_gather(feats_z, "y", axis=0, tiled=True)
    with jax.named_scope("cot_x"):
        cot_rows = lax.all_gather(cotangent, "x", axis=0, tiled=True)

    grads, keep, give = backward(
        tile_rows, dslot, tile_counts, coef, cot_rows, stacked, tile_values
    )
    with jax.named_scope("dx_c"):
        got = swap(give)
    dx = (keep + got.astype(F32)).reshape(NZ * NY * TILE, H)
    with jax.named_scope("dx_z"):
        dx = lax.psum_scatter(dx, "z", scatter_dimension=0, tiled=True)
    with jax.named_scope("dx_y"):
        dx = lax.psum_scatter(dx, "y", scatter_dimension=0, tiled=True)

    feats_mine = feats_mine.reshape(SLOTS, TILE, H)
    with jax.named_scope("feats_c"):
        feats_other = swap(feats_mine)
    rels = jnp.repeat(tile_rels, B)
    outp, dkeep, dgive, coefg = forward(
        tile_rows, xslot, tile_counts, mine[None], coef, rels[:, None], rels[None, :],
        feats_mine, feats_other, tile_values, grads, stacked, cot_rows,
    )

    with jax.named_scope("dv_c"):
        dgot = swap(dgive)
    dv = (dkeep + dgot[:1024].astype(F32)).reshape(NX, 256, H).astype(BF16)
    cg = coefg + dgot[1024:, :128].astype(F32) + dgot[1024:, 128:].astype(F32)
    cg_x = jnp.broadcast_to(two_parts(cg)[None], (NX, 32, H))
    with jax.named_scope("dv_x"):
        got_x = exchange(jnp.concatenate([dv, outp, cg_x], axis=1), "x")
    sum_x = jnp.sum(got_x.astype(F32), axis=0)
    layer_out = sum_x[256:384].astype(BF16)
    cg = sum_x[384:, :128] + sum_x[384:, 128:]
    pad = jnp.zeros((NY * NZ, 7, H), BF16)
    packed = jnp.concatenate(
        [sum_x[:256].reshape(NY * NZ, 8, H).astype(BF16), two_parts(cg)[:, None, :], pad], axis=1
    )
    with jax.named_scope("dv_yz"):
        got_yz = exchange(packed, ("y", "z"))
    sum_yz = jnp.sum(got_yz.astype(F32), axis=0)
    cg = sum_yz[8:9, :128] + sum_yz[8:9, 128:]
    packed = jnp.concatenate(
        [sum_yz[:8].astype(BF16), two_parts(cg), jnp.zeros((7, H), BF16)], axis=0
    )
    with jax.named_scope("all_yz"):
        all_yz = spread_to(packed, ("y", "z"), NY * NZ)
    scale = (NY * NZ * NC * NX * TILE) ** (-0.5)
    cg = all_yz[:, 8, :128].astype(F32) + all_yz[:, 8, 128:].astype(F32)
    grad_coef = (cg * scale).reshape(512, B)[:RELS]
    with jax.named_scope("all_x"):
        all_x = spread_to(all_yz[:, :8].reshape(256, H), "x", NX).reshape(1024, H)
    with jax.named_scope("all_c"):
        all_other = swap(all_x)
    first = jnp.where(mine == 0, all_x, all_other)
    second = jnp.where(mine == 0, all_other, all_x)
    grad_bases = (jnp.stack([first, second]).astype(F32) * scale).reshape(B, H, H)

    quotient = dx / counts[:, None]
    grad_entities = jnp.dot(member.astype(F32), quotient, precision=lax.Precision.HIGHEST)
    return (layer_out, grad_entities, grad_bases, grad_coef)


def solution(mesh):
    grid = Mesh(mesh.devices.reshape(NY, NZ, NC, NX), DEVICES)
    by_tile = P(DEVICES)
    by_class = P(("x",) + ROWS)
    placed = (
        by_class,
        by_class,
        by_tile,
        by_tile,
        by_tile,
        by_tile,
        by_tile,
        P(),
        P(),
        by_tile,
    )
    return jax.shard_map(
        local,
        mesh=grid,
        in_specs=placed,
        out_specs=(by_tile, by_class, P(), P()),
        check_vma=False,
    )
```

time: 571 us -> 192 us (0.34)
  waiting for transfers between devices: 391 us -> 37.8 us
  local copies, waits for them, and re-layouts: 32.2 us -> 5.35 us
  starting transfers between devices: 0.16 us -> 24.9 us
  Pallas kernels: 0 us -> 20.8 us
  blocking collectives: 86.7 us -> 68.9 us
  matrix products: 18.9 us -> 3.72 us
  other arithmetic: 22.2 us -> 12 us
    reduce_scatter x2, waiting for transfers between devices: 173 us -> 10.2 us  [the longest x1 10.2 us: local(): dx = lax.psum_scatter(dx, 'y', scatter_dimension=0, tiled=True)]
    psum x1 -> x0, waiting for transfers between devices: 148 us -> none  [local(): dv_sum, dcoef_sum = lax.psum((dv_part, dcoef_acc), ('row', 'col'))]
    psum x1 -> x0, blocking collectives: 75.5 us -> none  [local(): dv_sum, dcoef_sum = lax.psum((dv_part, dcoef_acc), ('row', 'col'))]
    all_gather x1, waiting for transfers between devices: 70.5 us -> 0.02 us  [local(): feats_mine = lax.all_gather(feats_z, 'y', axis=0, tiled=True)]
    all_to_all x0 -> x3, blocking collectives: none -> 58.5 us  [exchange(): return lax.all_to_all(x, axes, split_axis=0, concat_axis=0, tiled=True)]
    pallas_call x0 -> x2, Pallas kernels: none -> 20.8 us  [the longest x1 11.2 us: forward(): pl.pallas_call(forward_kernel, in_specs=[SMEM] * 5 + [VMEM] * 2 + [ANY] *...]
    all_to_all x0 -> x2, waiting for transfers between devices: none -> 18.8 us  [exchange(): return lax.all_to_all(x, axes, split_axis=0, concat_axis=0, tiled=True)]
    dot_general x11 -> x3, matrix products: 18.9 us -> 3.72 us  [the longest x1 1.95 us: local(): jnp.dot(member.astype(F32), quotient, precision=lax.Precision.HIGHEST)]
  transfers between devices with their start and end apart: 4 -> 9, of which waited for: 4 -> 6; matrix products, arithmetic and copies ran while one was open for 7% -> 8% of each run, Pallas kernels for 0% -> 11%
where the time goes in v1:
time: 192 us; the launch traced here: 190 us
  blocking collectives  68.9 us (36%)
  waiting for transfers between devices  37.8 us (20%)
  starting transfers between devices  24.9 us (13%)
  Pallas kernels  20.8 us (11%)
  between operations  16.4 us (9%)
  other arithmetic  12 us (6%)
  local copies, waits for them, and re-layouts  5.35 us (3%)
  matrix products  3.72 us (2%)
    all_to_all x3, blocking collectives, exchange(): return lax.all_to_all(x, axes, split_axis=0, concat_axis=0, tiled=True)  58.5 us
    all_to_all x2, waiting for transfers between devices, exchange(): return lax.all_to_all(x, axes, split_axis=0, concat_axis=0, tiled=True)  18.8 us
    all_to_all x2, starting transfers between devices, exchange(): return lax.all_to_all(x, axes, split_axis=0, concat_axis=0, tiled=True)  15 us
    pallas_call x1, Pallas kernels, forward(): pl.pallas_call(forward_kernel, in_specs=[SMEM] * 5 + [VMEM] * 2 + [ANY] *...  11.2 us
    all_gather x1, blocking collectives, local(): cot_rows = lax.all_gather(cotangent, 'x', axis=0, tiled=True)  10.4 us
    reduce_scatter x1, waiting for transfers between devices, local(): dx = lax.psum_scatter(dx, 'y', scatter_dimension=0, tiled=True)  10.2 us
    ppermute x4, starting transfers between devices, swap(): return lax.ppermute(x, 'c', [(0, 1), (1, 0)])  9.83 us
    pallas_call x1, Pallas kernels, backward(): pl.pallas_call(backward_kernel, in_specs=[SMEM, SMEM, SMEM, SMEM, VMEM, V...  9.66 us
  transfers between devices with their start and end apart: 9, of which 6 were waited for; matrix products, arithmetic and copies ran while one was open for 8% of the time, Pallas kernels for 11%

profile of v1, /device:TPU:1, one launch (start us, length us, event | category | flops | bytes accessed | tf_op | source)
XLA Modules:
  0.0 189.9 jit_solution(9088301479294859941)
XLA Ops:
  8.1 0.8 convert_reduce_fusion.2
  8.9 1.0 fusion
  9.9 24.9 %all_to_all.25 = bf16[8,128,256]{2,1,0:T(8,128)(2,1)} all-to-all(bf16[8,128,256]{2,1,0:T(8,128)(2,1)S(1)} %broadcast_in_dim.20), channel_id=1, replica_groups=mesh['y'=4,'z'=8,'c'=2,'x'=4] {'z'}, dimensions={0} | all-to-all | bytes 1048576 | tf_op jit(solution)/shard_map/feats_z/all_to_all | solution.py:177
  36.1 0.8 fusion.6.coef
  36.9 10.4 %all_gather.7.cot = bf16[512,256]{1,0:T(8,128)(2,1)} all-gather(bf16[128,256]{1,0:T(8,128)(2,1)S(1)} %copy-done.3), channel_id=1, replica_groups=mesh['y'=4,'z'=8,'c'=2,'x'=4] {'x'}, dimensions={0}, use_global_device_ids=true | all-gather | bytes 327680 | tf_op jit(solution)/shard_map/cot_x/all_gather | solution.py:228
  47.4 9.7 %backward.1 = (bf16[4,128,2048]{2,1,0:T(8,128)(2,1)}, f32[32,128,256]{2,1,0:T(8,128)}, bf16[32,128,256]{2,1,0:T(8,128)(2,1)}) custom-call(s32[32]{0:T(128)} %trow.3, s32[32]{0:T(128)} %get-tuple-element.34.dslot, s32[1]{0:T(128)S(6)} %copy.33.count, f32[32,8]{1,0:T(8,128)} %fusion.6.coef, bf16[512,256]{1,0:T(8,128)(2,1)} %all_gather.7.cot, ...), custom_call_target="tpu_custom_call" | custom-call | tf_op jit(solution)/shard_map/backward/pallas_call | solution.py:61
  57.0 4.2 %collective-permute-start.2 = (bf16[32,128,256]{2,1,0:T(8,128)(2,1)}, bf16[32,128,256]{2,1,0:T(8,128)(2,1)S(1)}, u32[]{:S(2)}, u32[]{:S(2)}) collective-permute-start(bf16[32,128,256]{2,1,0:T(8,128)(2,1)} %get-tuple-element.21), channel_id=1, source_target_pairs={{0,4},{4,0},{1,5},{5,1},{2,6},{6,2},{3,7},{7,3},{8,12},{12,8},{9,1... | collective-permute-start | bytes 6291464 | tf_op jit(solution)/shard_map/dx_c/ppermute | solution.py:173
  61.2 4.0 %collective-permute-done.2 = bf16[32,128,256]{2,1,0:T(8,128)(2,1)S(1)} collective-permute-done((bf16[32,128,256]{2,1,0:T(8,128)(2,1)}, bf16[32,128,256]{2,1,0:T(8,128)(2,1)S(1)}, u32[]{:S(2)}, u32[]{:S(2)}) %collective-permute-start.2) | collective-permute-done | bytes 2097184 | tf_op jit(solution)/shard_map/dx_c/ppermute | solution.py:173
  65.2 4.9 %convert_add_fusion = f32[32,128,256]{2,1,0:T(8,128)} fusion(f32[32,128,256]{2,1,0:T(8,128)} %get-tuple-element.20, bf16[32,128,256]{2,1,0:T(8,128)(2,1)S(1)} %collective-permute-done.2), kind=kLoop, calls=%fused_computation | loop fusion | flops 2097152 | bytes 10485760 | tf_op jit(solution)/shard_map/add | solution.py:235
  70.7 0.8 broadcast_in_dim_reshape.8.relc
  71.5 0.6 broadcast_in_dim_reshape.7.relr
  72.7 2.0 %collective-permute-done.xother = bf16[32,128,256]{2,1,0:T(8,128)(2,1)S(1)} collective-permute-done((bf16[32,128,256]{2,1,0:T(8,128)(2,1)}, bf16[32,128,256]{2,1,0:T(8,128)(2,1)S(1)}, u32[]{:S(2)}, u32[]{:S(2)}) %collective-permute-start) | collective-permute-done | bytes 2097184 | tf_op jit(solution)/shard_map/feats_c/ppermute | solution.py:173
  74.7 1.3 copy-done.1
  76.0 11.2 %forward.1 = (bf16[4,128,256]{2,1,0:T(8,128)(2,1)}, f32[1024,256]{1,0:T(8,128)}, bf16[1056,256]{1,0:T(8,128)(2,1)}, f32[32,128]{1,0:T(8,128)}) custom-call(s32[32]{0:T(128)} %trow.3, s32[32]{0:T(128)} %add_add_fusion.1.xslot, s32[1]{0:T(128)S(6)} %copy.33.count, s32[1]{0:T(128)} %bitcast.half, f32[32,8]{1,0:T(8,128)} %fusion.6.coef, ...), custom_call_target="tpu_custom_call" | custom-call | tf_op jit(solution)/shard_map/forward/pallas_call | solution.py:148
  87.3 2.1 %collective-permute-done.1 = bf16[1056,256]{1,0:T(8,128)(2,1)S(1)} collective-permute-done((bf16[1056,256]{1,0:T(8,128)(2,1)}, bf16[1056,256]{1,0:T(8,128)(2,1)S(1)}, u32[]{:S(2)}, u32[]{:S(2)}) %collective-permute-start.1) | collective-permute-done | bytes 540704 | tf_op jit(solution)/shard_map/dv_c/ppermute | solution.py:173
  89.4 0.7 reduce-precision_convert_fusion.1
  90.2 1.3 add_convert_fusion
  91.5 1.0 pad_maximum_fusion
  92.5 11.1 %all-to-all-start.1 = ((bf16[4,416,256]{2,1,0:T(8,128)(2,1)}), bf16[4,416,256]{2,1,0:T(8,128)(2,1)S(1)}, u32[]{:S(2)}, u32[]{:S(2)}) async-start(bf16[4,416,256]{2,1,0:T(8,128)(2,1)} %pad_maximum_fusion), calls=%async_computation.1 | async-start | bytes 1703936 | tf_op jit(solution)/shard_map/dv_x/all_to_all | solution.py:177
  103.7 12.6 %all-to-all-done.1 = bf16[4,416,256]{2,1,0:T(8,128)(2,1)S(1)} async-done(((bf16[4,416,256]{2,1,0:T(8,128)(2,1)}), bf16[4,416,256]{2,1,0:T(8,128)(2,1)S(1)}, u32[]{:S(2)}, u32[]{:S(2)}) %all-to-all-start.1) | async-done | bytes 852000 | tf_op jit(solution)/shard_map/dv_x/all_to_all | solution.py:177
  116.6 18.4 %all_to_all.26 = bf16[32,16,256]{2,1,0:T(8,128)(2,1)S(1)} all-to-all(bf16[32,16,256]{2,1,0:T(8,128)(2,1)S(1)} %maximum_maximum_fusion), channel_id=1, replica_groups=mesh['y'=4,'z'=8,'c'=2,'x'=4] {'y','z'}, dimensions={0} | all-to-all | bytes 524288 | tf_op jit(solution)/shard_map/dv_yz/all_to_all | solution.py:177
  135.1 15.2 %all_to_all.27 = bf16[32,16,256]{2,1,0:T(8,128)(2,1)S(1)} all-to-all(bf16[32,16,256]{2,1,0:T(8,128)(2,1)S(1)} %broadcast_in_dim.24), channel_id=1, replica_groups=mesh['y'=4,'z'=8,'c'=2,'x'=4] {'y','z'}, dimensions={0} | all-to-all | bytes 524288 | tf_op jit(solution)/shard_map/all_yz/all_to_all | solution.py:177
  150.3 0.8 broadcast_in_dim.52
  151.2 3.9 %all-to-all-start.4 = ((bf16[4,256,256]{2,1,0:T(8,128)(2,1)}), bf16[4,256,256]{2,1,0:T(8,128)(2,1)S(1)}, u32[]{:S(2)}, u32[]{:S(2)}) async-start(bf16[4,256,256]{2,1,0:T(8,128)(2,1)} %broadcast_in_dim.52), calls=%async_computation.6 | async-start | bytes 1048576 | tf_op jit(solution)/shard_map/all_x/all_to_all | solution.py:177
  155.1 0.7 reduce-scatter.5.cloned.1.call-update
  155.8 6.2 %all-to-all-done.4 = bf16[4,256,256]{2,1,0:T(8,128)(2,1)S(1)} async-done(((bf16[4,256,256]{2,1,0:T(8,128)(2,1)}), bf16[4,256,256]{2,1,0:T(8,128)(2,1)S(1)}, u32[]{:S(2)}, u32[]{:S(2)}) %all-to-all-start.4) | async-done | bytes 524320 | tf_op jit(solution)/shard_map/all_x/all_to_all | solution.py:177
  162.0 5.1 %collective-permute-start.3 = (bf16[1024,256]{1,0:T(8,128)(2,1)S(1)}, bf16[1024,256]{1,0:T(8,128)(2,1)S(1)}, u32[]{:S(2)}, u32[]{:S(2)}) collective-permute-start(bf16[1024,256]{1,0:T(8,128)(2,1)S(1)} %bitcast.29), channel_id=1, source_target_pairs={{0,4},{4,0},{1,5},{5,1},{2,6},{6,2},{3,7},{7,3},{8,12},{12,8},{9,1... | collective-permute-start | bytes 1572872 | tf_op jit(solution)/shard_map/all_c/ppermute | solution.py:173
  167.1 0.6 slice.62
  168.0 0.7 copy.31
  168.8 1.5 convert_multiply_fusion
  170.3 10.2 %reduce-scatter.5.cloned.1.call-done = f32[128,256]{1,0:T(8,128)} async-done(((f32[512,256]{1,0:T(8,128)}), f32[128,256]{1,0:T(8,128)}) %reduce-scatter.5.cloned.1.call-update) | async-done | bytes 131088 | tf_op jit(solution)/shard_map/dx_y/reduce_scatter | solution.py:239
  180.5 2.0 %fusion.1 = f32[256,256]{1,0:T(8,128)} fusion(f32[128,256]{1,0:T(8,128)} %reduce-scatter.5.cloned.1.call-done, f32[128]{0:T(128)S(1)} %convert_reduce_fusion.2, s32[256]{0:T(256)S(1)} %copy-done.7), kind=kOutput, calls=%fused_computation.13 | convolution fusion | flops 100728832 | bytes 394752 | tf_op jit(solution)/shard_map/dot_general | solution.py:285
  (50 shorter events, 2.8 us)
Async XLA Ops:
  8.0 0.9 copy-start
  8.0 28.9 %copy-start.3 = (bf16[128,256]{1,0:T(8,128)(2,1)S(1)}, bf16[128,256]{1,0:T(8,128)(2,1)}, u32[]{:S(2)}) copy-start(bf16[128,256]{1,0:T(8,128)(2,1)} %param.19) | copy-start | bytes 196612
  8.0 27.6 %copy-start.5 = (s32[32]{0:T(128)S(1)}, s32[32]{0:T(128)}, u32[]{:S(2)}) copy-start(s32[32]{0:T(128)} %param.14) | copy-start | bytes 388
  8.0 28.1 %copy-start.4 = (s32[32]{0:T(128)S(1)}, s32[32]{0:T(128)}, u32[]{:S(2)}) copy-start(s32[32]{0:T(128)} %param.15) | copy-start | bytes 388
  8.0 28.1 %copy-start.6 = (bf16[500,8]{0,1:T(8,128)(2,1)S(1)}, bf16[500,8]{0,1:T(8,128)(2,1)}, u32[]{:S(2)}) copy-start(bf16[500,8]{0,1:T(8,128)(2,1)} %param.17) | copy-start | bytes 24004
  8.1 62.1 %all-gather.2.cloned.1.call-start = ((), (), s32[]{:S(2)}) async-start(), calls=%async_computation.7 | async-start | bytes 2621440 | tf_op jit(solution)/shard_map/feats_y/all_gather | solution.py:226
  34.9 120.2 %reduce-scatter.3.cloned.1.call-start = ((), (), s32[]{:S(2)}) async-start(), calls=%async_computation.8 | async-start | bytes 4718592 | tf_op jit(solution)/shard_map/dx_z/reduce_scatter | solution.py:237
  57.0 8.2 %collective-permute-start.2 = (bf16[32,128,256]{2,1,0:T(8,128)(2,1)}, bf16[32,128,256]{2,1,0:T(8,128)(2,1)S(1)}, u32[]{:S(2)}, u32[]{:S(2)}) collective-permute-start(bf16[32,128,256]{2,1,0:T(8,128)(2,1)} %get-tuple-element.21), channel_id=1, source_target_pairs={{0,4},{4,0},{1,5},{5,1},{2,6},{6,2},{3,7},{7,3},{8,12},{12,8},{9,1... | collective-permute-start | bytes 6291464 | tf_op jit(solution)/shard_map/dx_c/ppermute | solution.py:173
  70.2 4.5 %collective-permute-start = (bf16[32,128,256]{2,1,0:T(8,128)(2,1)}, bf16[32,128,256]{2,1,0:T(8,128)(2,1)S(1)}, u32[]{:S(2)}, u32[]{:S(2)}) collective-permute-start(bf16[32,128,256]{2,1,0:T(8,128)(2,1)} %bitcast.27), channel_id=1, source_target_pairs={{0,4},{4,0},{1,5},{5,1},{2,6},{6,2},{3,7},{7,3},{8,12},{12,8},{9,1... | collective-permute-start | bytes 6291464 | tf_op jit(solution)/shard_map/feats_c/ppermute | solution.py:173
  74.7 1.3 copy-start.1
  87.2 4.3 %copy-start.2 = (bf16[4,128,256]{2,1,0:T(8,128)(2,1)S(1)}, bf16[4,128,256]{2,1,0:T(8,128)(2,1)}, u32[]{:S(2)}) copy-start(bf16[4,128,256]{2,1,0:T(8,128)(2,1)} %get-tuple-element.18) | copy-start | bytes 786436
  87.2 2.2 %collective-permute-start.1 = (bf16[1056,256]{1,0:T(8,128)(2,1)}, bf16[1056,256]{1,0:T(8,128)(2,1)S(1)}, u32[]{:S(2)}, u32[]{:S(2)}) collective-permute-start(bf16[1056,256]{1,0:T(8,128)(2,1)} %get-tuple-element.17), channel_id=1, source_target_pairs={{0,4},{4,0},{1,5},{5,1},{2,6},{6,2},{3,7},{7,3},{8,12},{12,8},{9,1... | collective-permute-start | bytes 1622024 | tf_op jit(solution)/shard_map/dv_c/ppermute | solution.py:173
  92.5 23.8 %all-to-all-start.1 = ((bf16[4,416,256]{2,1,0:T(8,128)(2,1)}), bf16[4,416,256]{2,1,0:T(8,128)(2,1)S(1)}, u32[]{:S(2)}, u32[]{:S(2)}) async-start(bf16[4,416,256]{2,1,0:T(8,128)(2,1)} %pad_maximum_fusion), calls=%async_computation.1 | async-start | bytes 1703936 | tf_op jit(solution)/shard_map/dv_x/all_to_all | solution.py:177
  151.2 10.8 %all-to-all-start.4 = ((bf16[4,256,256]{2,1,0:T(8,128)(2,1)}), bf16[4,256,256]{2,1,0:T(8,128)(2,1)S(1)}, u32[]{:S(2)}, u32[]{:S(2)}) async-start(bf16[4,256,256]{2,1,0:T(8,128)(2,1)} %broadcast_in_dim.52), calls=%async_computation.6 | async-start | bytes 1048576 | tf_op jit(solution)/shard_map/all_x/all_to_all | solution.py:177
  155.1 25.4 %reduce-scatter.5.cloned.1.call-start = ((), (), s32[]{:S(2)}) async-start(), calls=%async_computation.9 | async-start | bytes 655360 | tf_op jit(solution)/shard_map/dx_y/reduce_scatter | solution.py:239
  162.0 6.7 %collective-permute-start.3 = (bf16[1024,256]{1,0:T(8,128)(2,1)S(1)}, bf16[1024,256]{1,0:T(8,128)(2,1)S(1)}, u32[]{:S(2)}, u32[]{:S(2)}) collective-permute-start(bf16[1024,256]{1,0:T(8,128)(2,1)S(1)} %bitcast.29), channel_id=1, source_target_pairs={{0,4},{4,0},{1,5},{5,1},{2,6},{6,2},{3,7},{7,3},{8,12},{12,8},{9,1... | collective-permute-start | bytes 1572872 | tf_op jit(solution)/shard_map/all_c/ppermute | solution.py:173
  168.8 11.7 %copy-start.7 = (s32[256]{0:T(256)S(1)}, s32[256]{0:T(256)}, u32[]{:S(2)}) copy-start(s32[256]{0:T(256)} %param.11) | copy-start | bytes 3076
Sparse Core Ops, SparseCore 0:
  35.0 31.5 all-gather.1
  158.4 22.0 reduce-scatter.4
Sparse Core Ops, SparseCore 1:
  70.3 56.0 reduce-scatter.2

commit v2 on v1

v2 whole, which is shorter than its diff:
```python
import jax
import jax.numpy as jnp
from jax import lax
from jax.experimental import pallas as pl
from jax.experimental.pallas import tpu as pltpu
from jax.sharding import Mesh
from jax.sharding import PartitionSpec as P

NY, NZ, NC, NX = 4, 8, 2, 4
TILE = 128
H = 256
B = 8
SLOTS = 32
TROWS = 4
RELS = 500
F32, BF16 = jnp.float32, jnp.bfloat16
ROWS = ("y", "z", "c")
DEVICES = ("y", "z", "c", "x")
VMEM = pl.BlockSpec(memory_space=pltpu.VMEM)
SMEM = pl.BlockSpec(memory_space=pltpu.SMEM)
ANY = pl.BlockSpec(memory_space=pl.ANY)
PARAMS = pltpu.CompilerParams(vmem_limit_bytes=56 * 2**20)


def by_row(trow, count, order, filled):
    for t in range(TROWS):
        filled[t] = 0

    def put(s, carry):
        t = trow[s]
        n = filled[t]
        order[t, n] = s
        filled[t] = n + 1
        return carry

    lax.fori_loop(0, count[0], put, 0)
    for t in range(TROWS):
        order[t, filled[t]] = SLOTS


def pairs(order, filled, body):
    def row(t, carry):
        def pair(p, inner):
            body(t, order[t, 2 * p], order[t, 2 * p + 1])
            return inner

        lax.fori_loop(0, (filled[t] + 1) // 2, pair, 0)
        return carry

    lax.fori_loop(0, TROWS, row, 0)


def fold(x):
    return (x[:8, :128] + x[:8, 128:]) + (x[8:, :128] + x[8:, 128:])


def fours(count, body):
    def group(q, carry):
        for k in range(4):
            body(4 * q + k)
        return carry

    lax.fori_loop(0, (count[0] + 3) // 4, group, 0)


def backward_kernel(
    trow, dslot, count, coef, cot_in, bases_in, tiles_in, grads_out, keep_out, give_out,
    cot, bases, tiles, wide, grads, total, mixed, narrow, order, filled, sems,
):
    loads = [
        pltpu.make_async_copy(src, dst, sems.at[k])
        for k, (src, dst) in enumerate(((cot_in, cot), (bases_in, bases), (tiles_in, tiles)))
    ]
    for copy in loads:
        copy.start()
    total[...] = jnp.zeros_like(total)
    mixed[...] = jnp.zeros_like(mixed)
    by_row(trow, count, order, filled)
    loads[0].wait()
    loads[1].wait()
    for b in range(B):
        g = lax.dot_general(
            cot[...], bases[pl.ds(b * H, H), :], (((1,), (1,)), ((), ())), preferred_element_type=F32
        ).astype(BF16)
        grads[:, b] = g.reshape(TROWS, TILE, H)
        wide[:, b] = g.astype(F32).reshape(TROWS, TILE, H)
    store = pltpu.make_async_copy(grads, grads_out, sems.at[3])
    store.start()

    def mix(t, s1, s2):
        c1 = [coef[s1, b] for b in range(B)]
        c2 = [coef[s2, b] for b in range(B)]
        for r in range(4):
            rows = pl.ds(r * 32, 32)
            g = wide[t, 0, rows, :]
            m1 = c1[0] * g
            m2 = c2[0] * g
            for b in range(1, B):
                g = wide[t, b, rows, :]
                m1 = m1 + c1[b] * g
                m2 = m2 + c2[b] * g
            mixed[s1, rows, :] = m1.astype(BF16)
            mixed[s2, rows, :] = m2.astype(BF16)

    pairs(order, filled, mix)
    loads[2].wait()

    def back(s):
        d = dslot[s]
        total[d] = total[d] + lax.dot_general(
            tiles[s], mixed[s], (((0,), (0,)), ((), ())), preferred_element_type=F32
        )

    fours(count, back)
    outs = []
    for k, out in ((1, give_out), (0, keep_out)):
        narrow[k] = total[pl.ds(k * SLOTS, SLOTS)].astype(BF16)
        copy = pltpu.make_async_copy(narrow.at[k], out, sems.at[4 + k])
        copy.start()
        outs.append(copy)
    store.wait()
    for copy in outs:
        copy.wait()


def backward(trow, dslot, count, coef, cot_rows, stacked, tile_values):
    blocks = jax.ShapeDtypeStruct((SLOTS, TILE, H), BF16)
    return pl.pallas_call(
        backward_kernel,
        in_specs=[SMEM] * 4 + [ANY] * 3,
        out_specs=[ANY] * 3,
        out_shape=[jax.ShapeDtypeStruct((TROWS, B, TILE, H), BF16), blocks, blocks],
        scratch_shapes=[
            pltpu.VMEM((TROWS * TILE, H), BF16),
            pltpu.VMEM((B * H, H), BF16),
            pltpu.VMEM((SLOTS, TILE, TILE), BF16),
            pltpu.VMEM((TROWS, B, TILE, H), F32),
            pltpu.VMEM((TROWS, B, TILE, H), BF16),
            pltpu.VMEM((2 * SLOTS, TILE, H), F32),
            pltpu.VMEM((SLOTS + 1, TILE, H), BF16),
            pltpu.VMEM((2, SLOTS, TILE, H), BF16),
            pltpu.SMEM((TROWS, SLOTS + 8), jnp.int32),
            pltpu.SMEM((TROWS,), jnp.int32),
            pltpu.SemaphoreType.DMA((6,)),
        ],
        compiler_params=PARAMS,
        name="backward",
    )(trow, dslot, count, coef, cot_rows, stacked, tile_values)


def forward_kernel(
    trow, xslot, count, half, coef, relc, relr, xmine, xother, tiles_in, grads_in, bases_in, cot_in,
    outp, dkeep, dgive, coefg,
    feats, tiles, grads, bases, cot, sums, part, msg, gram, order, filled, sems,
):
    loads = [
        pltpu.make_async_copy(src, dst, sems.at[k])
        for k, (src, dst) in enumerate(
            (
                (tiles_in, tiles),
                (xmine, feats.at[pl.ds(0, SLOTS)]),
                (xother, feats.at[pl.ds(SLOTS, SLOTS)]),
                (grads_in, grads),
                (bases_in, bases),
                (cot_in, cot),
            )
        )
    ]
    for copy in loads:
        copy.start()
    sums[...] = jnp.zeros_like(sums)
    msg[SLOTS] = jnp.zeros((TILE, H), F32)
    gram[...] = jnp.zeros_like(gram)
    by_row(trow, count, order, filled)
    for copy in loads[:4]:
        copy.wait()
    def message(s):
        m = jnp.dot(tiles[s], feats[xslot[s]], preferred_element_type=F32).astype(BF16)
        msg[s] = m.astype(F32)

    fours(count, message)

    def add(t, s1, s2):
        c1 = [coef[s1, b] for b in range(B)]
        c2 = [coef[s2, b] for b in range(B)]
        d1 = [jnp.zeros((8, 128), F32)] * B
        d2 = [jnp.zeros((8, 128), F32)] * B
        for r in range(8):
            rows = pl.ds(r * 16, 16)
            m1 = msg[s1, rows, :]
            m2 = msg[s2, rows, :]
            for b in range(B):
                sums[t, b, rows, :] = sums[t, b, rows, :] + (c1[b] * m1 + c2[b] * m2)
                g = grads[t, b, rows, :].astype(F32)
                d1[b] = d1[b] + fold(m1 * g)
                d2[b] = d2[b] + fold(m2 * g)
        for b in range(B):
            gram[s1, b] = d1[b]
            gram[s2, b] = d2[b]

    pairs(order, filled, add)

    for copy in loads[4:]:
        copy.wait()
    for t in range(TROWS):
        for b in range(B):
            part[pl.ds(t * TILE, TILE), pl.ds(b * H, H)] = sums[t, b].astype(BF16)
    outp[...] = jnp.dot(part[...], bases[...], preferred_element_type=F32).astype(BF16)
    mine = half[0]

    def outer(k):
        cols = pl.ds(pl.multiple_of(k * H, H), H)
        return lax.dot_general(
            part[:, cols], cot[...], (((0,), (0,)), ((), ())), preferred_element_type=F32
        )

    for k in range(B // 2):
        rows = pl.ds(k * H, H)
        dkeep[rows, :] = outer(mine * (B // 2) + k)
        dgive[rows, :] = outer((1 - mine) * (B // 2) + k).astype(BF16)

    col = jnp.sum(jnp.sum(gram[pl.ds(0, SLOTS)].reshape(SLOTS * B, 8, 128), axis=1), axis=1, keepdims=True)
    lane = lax.broadcasted_iota(jnp.int32, (SLOTS * B, 128), 1)
    row = lax.broadcasted_iota(jnp.int32, (SLOTS * B, 128), 0)
    pick = (lane % B == row % B) & (lane // B == relc[...] % 16) & (row < count[0] * B)
    spread = jnp.where(pick, col, 0.0)
    line = lax.broadcasted_iota(jnp.int32, (32, SLOTS * B), 0)
    gather = (relr[...] // 16 == line).astype(F32)
    cg = jnp.dot(gather, spread, precision=lax.Precision.HIGHEST, preferred_element_type=F32)
    coefg[...] = cg
    hi = cg.astype(BF16)
    dgive[pl.ds(1024, 32), pl.ds(0, 128)] = hi
    dgive[pl.ds(1024, 32), pl.ds(128, 128)] = (cg - hi.astype(F32)).astype(BF16)


def forward(trow, xslot, count, half, coef, relc, relr, xmine, xother, tiles, grads, stacked, cot_rows):
    return pl.pallas_call(
        forward_kernel,
        in_specs=[SMEM] * 5 + [VMEM] * 2 + [ANY] * 6,
        out_specs=[VMEM] * 4,
        out_shape=[
            jax.ShapeDtypeStruct((TROWS * TILE, H), BF16),
            jax.ShapeDtypeStruct((1024, H), F32),
            jax.ShapeDtypeStruct((1056, H), BF16),
            jax.ShapeDtypeStruct((32, 128), F32),
        ],
        scratch_shapes=[
            pltpu.VMEM((2 * SLOTS, TILE, H), BF16),
            pltpu.VMEM((SLOTS, TILE, TILE), BF16),
            pltpu.VMEM((TROWS, B, TILE, H), BF16),
            pltpu.VMEM((B * H, H), BF16),
            pltpu.VMEM((TROWS * TILE, H), BF16),
            pltpu.VMEM((TROWS, B, TILE, H), F32),
            pltpu.VMEM((TROWS * TILE, B * H), BF16),
            pltpu.VMEM((SLOTS + 1, TILE, H), F32),
            pltpu.VMEM((SLOTS + 1, B, 8, 128), F32),
            pltpu.SMEM((TROWS, SLOTS + 8), jnp.int32),
            pltpu.SMEM((TROWS,), jnp.int32),
            pltpu.SemaphoreType.DMA((6,)),
        ],
        compiler_params=PARAMS,
        name="forward",
    )(trow, xslot, count, half, coef, relc, relr, xmine, xother, tiles, grads, stacked, cot_rows)


def swap(x):
    return lax.ppermute(x, "c", [(0, 1), (1, 0)])


def exchange(x, axes):
    return lax.all_to_all(x, axes, split_axis=0, concat_axis=0, tiled=True)


def spread_to(x, axes, n):
    return exchange(jnp.broadcast_to(x[None], (n,) + x.shape), axes)


def two_parts(x):
    hi = lax.reduce_precision(x, 8, 7)
    return jnp.concatenate([hi, x - hi], axis=-1).astype(BF16)


def after(x, y):
    return lax.optimization_barrier((x, y))


def local(
    entity_feats,
    class_map,
    tile_values,
    tile_rows,
    tile_column_index,
    tile_rels,
    tile_counts,
    coefficients,
    bases,
    cotangent,
):
    mine = lax.axis_index("c").astype(jnp.int32)
    member = class_map[:, None] == jnp.arange(TILE, dtype=jnp.int32)[None, :]
    sums = lax.dot_general(
        member.astype(BF16), entity_feats, (((0,), (0,)), ((), ())), preferred_element_type=F32
    )
    counts = jnp.sum(member.astype(F32), axis=0)
    class_feat = (sums / counts[:, None]).astype(BF16)

    rels = jnp.pad(tile_rels, (0, 8), constant_values=-1)
    pick_rel = (rels[:, None] == jnp.arange(RELS, dtype=jnp.int32)[None, :]).astype(BF16)
    coef = jnp.dot(pick_rel, coefficients, preferred_element_type=F32)
    other = (tile_column_index % 2 != mine).astype(jnp.int32) * SLOTS
    ty = tile_column_index // (2 * NZ)
    tz = (tile_column_index // 2) % NZ
    xslot = other + ty * NZ + tz
    dslot = other + tz * NY + ty
    stacked = bases.reshape(B * H, H)

    with jax.named_scope("feats_z"):
        feats_z = spread_to(class_feat, "z", NZ).reshape(NZ * TILE, H)
    cotangent, feats_z = after(cotangent, feats_z)
    with jax.named_scope("feats_y"):
        feats_mine = lax.all_gather(feats_z, "y", axis=0, tiled=True)
    with jax.named_scope("cot_x"):
        cot_rows = lax.all_gather(cotangent, "x", axis=0, tiled=True)

    grads, keep, give = backward(
        tile_rows, dslot, tile_counts, coef, cot_rows, stacked, tile_values
    )
    with jax.named_scope("dx_c"):
        got = swap(give)
    dx = (keep.astype(F32) + got.astype(F32)).reshape(NZ * NY * TILE, H)
    with jax.named_scope("dx_z"):
        dx = lax.psum_scatter(dx, "z", scatter_dimension=0, tiled=True)
    feats_mine = feats_mine.reshape(SLOTS, TILE, H)
    with jax.named_scope("feats_c"):
        feats_other = swap(feats_mine)
    rels = jnp.repeat(tile_rels, B)
    outp, dkeep, dgive, coefg = forward(
        tile_rows, xslot, tile_counts, mine[None], coef, rels[:, None], rels[None, :],
        feats_mine, feats_other, tile_values, grads, stacked, cot_rows,
    )

    with jax.named_scope("dv_c"):
        dgot = swap(dgive)
    dv = (dkeep + dgot[:1024].astype(F32)).reshape(NX, 256, H).astype(BF16)
    cg = coefg + dgot[1024:, :128].astype(F32) + dgot[1024:, 128:].astype(F32)
    cg_x = jnp.broadcast_to(two_parts(cg)[None], (NX, 32, H))
    with jax.named_scope("dv_x"):
        got_x = exchange(jnp.concatenate([dv, outp.reshape(NX, TILE, H), cg_x], axis=1), "x")
    sum_x = jnp.sum(got_x.astype(F32), axis=0)
    layer_out = sum_x[256:384].astype(BF16)
    cg = sum_x[384:, :128] + sum_x[384:, 128:]
    pad = jnp.zeros((NY * NZ, 7, H), BF16)
    packed = jnp.concatenate(
        [sum_x[:256].reshape(NY * NZ, 8, H).astype(BF16), two_parts(cg)[:, None, :], pad], axis=1
    )
    with jax.named_scope("dv_yz"):
        got_yz = exchange(packed, ("y", "z"))
    sum_yz = jnp.sum(got_yz.astype(F32), axis=0)
    cg = sum_yz[8:9, :128] + sum_yz[8:9, 128:]
    packed = jnp.concatenate(
        [sum_yz[:8].astype(BF16), two_parts(cg), jnp.zeros((7, H), BF16)], axis=0
    )
    packed, dx = after(packed, dx)
    with jax.named_scope("dx_y"):
        dx = lax.psum_scatter(dx, "y", scatter_dimension=0, tiled=True)
    with jax.named_scope("all_yz"):
        all_yz = spread_to(packed, ("y", "z"), NY * NZ)
    scale = (NY * NZ * NC * NX * TILE) ** (-0.5)
    cg = all_yz[:, 8, :128].astype(F32) + all_yz[:, 8, 128:].astype(F32)
    grad_coef = (cg * scale).reshape(512, B)[:RELS]
    with jax.named_scope("all_x"):
        all_x = spread_to(all_yz[:, :8].reshape(256, H), "x", NX).reshape(1024, H)
    with jax.named_scope("all_c"):
        all_other = swap(all_x)
    first = jnp.where(mine == 0, all_x, all_other)
    second = jnp.where(mine == 0, all_other, all_x)
    grad_bases = (jnp.stack([first, second]).astype(F32) * scale).reshape(B, H, H)

    quotient = dx / counts[:, None]
    grad_entities = jnp.dot(member.astype(F32), quotient, precision=lax.Precision.HIGHEST)
    return (layer_out, grad_entities, grad_bases, grad_coef)


def solution(mesh):
    grid = Mesh(mesh.devices.reshape(NY, NZ, NC, NX), DEVICES)
    by_tile = P(DEVICES)
    by_class = P(("x",) + ROWS)
    placed = (
        by_class,
        by_class,
        by_tile,
        by_tile,
        by_tile,
        by_tile,
        by_tile,
        P(),
        P(),
        by_tile,
    )
    return jax.shard_map(
        local,
        mesh=grid,
        in_specs=placed,
        out_specs=(by_tile, by_class, P(), P()),
        check_vma=False,
    )
```

time: 192 us -> 174 us (0.906)
  waiting for transfers between devices: 37.8 us -> 30.8 us
  Pallas kernels: 20.8 us -> 14.9 us
  blocking collectives: 68.9 us -> 63.7 us
    reduce_scatter x1, waiting for transfers between devices: 10.2 us -> 0.79 us  [local(): dx = lax.psum_scatter(dx, 'y', scatter_dimension=0, tiled=True)]
    all_to_all x3, blocking collectives: 58.5 us -> 53.3 us  [exchange(): return lax.all_to_all(x, axes, split_axis=0, concat_axis=0, tiled=True)]
    pallas_call x1, Pallas kernels: 9.66 us -> 6.11 us  [backward(): pl.pallas_call(backward_kernel, in_specs=[SMEM] * 4 + [ANY] * 3, out_spec...]
    all_to_all x2, waiting for transfers between devices: 18.8 us -> 21.5 us  [exchange(): return lax.all_to_all(x, axes, split_axis=0, concat_axis=0, tiled=True)]
    ppermute x4, starting transfers between devices: 9.83 us -> 12.2 us  [swap(): return lax.ppermute(x, 'c', [(0, 1), (1, 0)])]
    pallas_call x1, Pallas kernels: 11.2 us -> 8.82 us  [forward(): pl.pallas_call(forward_kernel, in_specs=[SMEM] * 5 + [VMEM] * 2 + [ANY] *...]
  transfers between devices with their start and end apart: 9 -> 9, of which waited for: 6 -> 6; matrix products, arithmetic and copies ran while one was open for 8% -> 9% of each run, Pallas kernels for 11% -> 9%
where the time goes in v2:
time: 174 us; the launch traced here: 172 us
  blocking collectives  63.7 us (37%)
  waiting for transfers between devices  30.8 us (18%)
  starting transfers between devices  26.3 us (15%)
  between operations  16.4 us (9%)
  Pallas kernels  14.9 us (9%)
  other arithmetic  11.2 us (6%)
  local copies, waits for them, and re-layouts  5.3 us (3%)
  matrix products  3.73 us (2%)
    all_to_all x3, blocking collectives, exchange(): return lax.all_to_all(x, axes, split_axis=0, concat_axis=0, tiled=True)  53.3 us
    all_to_all x2, waiting for transfers between devices, exchange(): return lax.all_to_all(x, axes, split_axis=0, concat_axis=0, tiled=True)  21.5 us
    all_to_all x2, starting transfers between devices, exchange(): return lax.all_to_all(x, axes, split_axis=0, concat_axis=0, tiled=True)  13.9 us
    ppermute x4, starting transfers between devices, swap(): return lax.ppermute(x, 'c', [(0, 1), (1, 0)])  12.2 us
    all_gather x1, blocking collectives, local(): cot_rows = lax.all_gather(cotangent, 'x', axis=0, tiled=True)  10.4 us
    pallas_call x1, Pallas kernels, forward(): pl.pallas_call(forward_kernel, in_specs=[SMEM] * 5 + [VMEM] * 2 + [ANY] *...  8.82 us
    ppermute x4, waiting for transfers between devices, swap(): return lax.ppermute(x, 'c', [(0, 1), (1, 0)])  7.76 us
    pallas_call x1, Pallas kernels, backward(): pl.pallas_call(backward_kernel, in_specs=[SMEM] * 4 + [ANY] * 3, out_spec...  6.11 us
  transfers between devices with their start and end apart: 9, of which 6 were waited for; matrix products, arithmetic and copies ran while one was open for 9% of the time, Pallas kernels for 9%

profile of v2, /device:TPU:1, one launch (start us, length us, event | category | flops | bytes accessed | tf_op | source)
XLA Modules:
  0.0 172.3 jit_solution(2985786043615044522)
XLA Ops:
  8.1 0.8 convert_reduce_fusion.2
  8.9 1.0 fusion
  9.9 24.9 %all_to_all.25 = bf16[8,128,256]{2,1,0:T(8,128)(2,1)} all-to-all(bf16[8,128,256]{2,1,0:T(8,128)(2,1)S(1)} %broadcast_in_dim.20), channel_id=1, replica_groups=mesh['y'=4,'z'=8,'c'=2,'x'=4] {'z'}, dimensions={0} | all-to-all | bytes 1048576 | tf_op jit(solution)/shard_map/feats_z/all_to_all | solution.py:271
  36.2 0.8 fusion.3.coef
  37.0 10.4 %all_gather.7.cot_in = bf16[512,256]{1,0:T(8,128)(2,1)} all-gather(bf16[128,256]{1,0:T(8,128)(2,1)S(1)} %copy-done.3), channel_id=1, replica_groups=mesh['y'=4,'z'=8,'c'=2,'x'=4] {'x'}, dimensions={0}, use_global_device_ids=true | all-gather | bytes 327680 | tf_op jit(solution)/shard_map/cot_x/all_gather | solution.py:323
  47.4 6.1 %backward.1 = (bf16[4,8,128,256]{3,2,1,0:T(8,128)(2,1)}, bf16[32,128,256]{2,1,0:T(8,128)(2,1)}, bf16[32,128,256]{2,1,0:T(8,128)(2,1)}) custom-call(s32[32]{0:T(128)} %trow.3, s32[32]{0:T(128)} %get-tuple-element.38.dslot, s32[1]{0:T(128)S(6)} %copy.33.count, f32[40,8]{1,0:T(8,128)} %fusion.3.coef, bf16[512,256]{1,0:T(8,128)(2,1)} %all_gather.7.cot_in, ...), custom_call_target="tpu_custom_call" | custom-call | tf_op jit(solution)/shard_map/backward/pallas_call | solution.py:128
  53.5 5.9 %collective-permute-start.2 = (bf16[32,128,256]{2,1,0:T(8,128)(2,1)}, bf16[32,128,256]{2,1,0:T(8,128)(2,1)S(1)}, u32[]{:S(2)}, u32[]{:S(2)}) collective-permute-start(bf16[32,128,256]{2,1,0:T(8,128)(2,1)} %get-tuple-element.23), channel_id=1, source_target_pairs={{0,4},{4,0},{1,5},{5,1},{2,6},{6,2},{3,7},{7,3},{8,12},{12,8},{9,1... | collective-permute-start | bytes 6291464 | tf_op jit(solution)/shard_map/dx_c/ppermute | solution.py:267
  59.4 4.0 %collective-permute-done.2 = bf16[32,128,256]{2,1,0:T(8,128)(2,1)S(1)} collective-permute-done((bf16[32,128,256]{2,1,0:T(8,128)(2,1)}, bf16[32,128,256]{2,1,0:T(8,128)(2,1)S(1)}, u32[]{:S(2)}, u32[]{:S(2)}) %collective-permute-start.2) | collective-permute-done | bytes 2097184 | tf_op jit(solution)/shard_map/dx_c/ppermute | solution.py:267
  63.4 4.2 %convert_add_fusion = f32[32,128,256]{2,1,0:T(8,128)} fusion(bf16[32,128,256]{2,1,0:T(8,128)(2,1)S(1)} %collective-permute-done.2, bf16[32,128,256]{2,1,0:T(8,128)(2,1)} %get-tuple-element.22), kind=kLoop, calls=%fused_computation | loop fusion | flops 3145728 | bytes 8388608 | tf_op jit(solution)/shard_map/add | solution.py:330
  68.3 0.8 broadcast_in_dim_reshape.8.relc
  69.0 0.7 broadcast_in_dim_reshape.7.relr
  70.2 2.0 %collective-permute-done.xother = bf16[32,128,256]{2,1,0:T(8,128)(2,1)S(1)} collective-permute-done((bf16[32,128,256]{2,1,0:T(8,128)(2,1)}, bf16[32,128,256]{2,1,0:T(8,128)(2,1)S(1)}, u32[]{:S(2)}, u32[]{:S(2)}) %collective-permute-start) | collective-permute-done | bytes 2097184 | tf_op jit(solution)/shard_map/feats_c/ppermute | solution.py:267
  72.2 1.3 copy-done.1
  73.5 8.8 %forward.1 = (bf16[512,256]{1,0:T(8,128)(2,1)}, f32[1024,256]{1,0:T(8,128)}, bf16[1056,256]{1,0:T(8,128)(2,1)}, f32[32,128]{1,0:T(8,128)}) custom-call(s32[32]{0:T(128)} %trow.3, s32[32]{0:T(128)} %add_add_fusion.1.xslot, s32[1]{0:T(128)S(6)} %copy.33.count, s32[1]{0:T(128)} %bitcast.half, f32[40,8]{1,0:T(8,128)} %fusion.3.coef, ...), custom_call_target="tpu_custom_call" | custom-call | tf_op jit(solution)/shard_map/forward/pallas_call | solution.py:237
  82.4 0.8 collective-permute-start.1
  83.1 1.8 %collective-permute-done.1 = bf16[1056,256]{1,0:T(8,128)(2,1)S(1)} collective-permute-done((bf16[1056,256]{1,0:T(8,128)(2,1)}, bf16[1056,256]{1,0:T(8,128)(2,1)S(1)}, u32[]{:S(2)}, u32[]{:S(2)}) %collective-permute-start.1) | collective-permute-done | bytes 540704 | tf_op jit(solution)/shard_map/dv_c/ppermute | solution.py:267
  84.9 0.7 reduce-precision_convert_fusion.1
  85.6 1.4 add_convert_fusion
  87.0 1.0 pad_maximum_fusion
  88.0 7.6 %all-to-all-start.1 = ((bf16[4,416,256]{2,1,0:T(8,128)(2,1)}), bf16[4,416,256]{2,1,0:T(8,128)(2,1)S(1)}, u32[]{:S(2)}, u32[]{:S(2)}) async-start(bf16[4,416,256]{2,1,0:T(8,128)(2,1)} %pad_maximum_fusion), calls=%async_computation.1 | async-start | bytes 1703936 | tf_op jit(solution)/shard_map/dv_x/all_to_all | solution.py:271
  95.6 12.6 %all-to-all-done.1 = bf16[4,416,256]{2,1,0:T(8,128)(2,1)S(1)} async-done(((bf16[4,416,256]{2,1,0:T(8,128)(2,1)}), bf16[4,416,256]{2,1,0:T(8,128)(2,1)S(1)}, u32[]{:S(2)}, u32[]{:S(2)}) %all-to-all-start.1) | async-done | bytes 852000 | tf_op jit(solution)/shard_map/dv_x/all_to_all | solution.py:271
  108.6 18.9 %all_to_all.26 = bf16[32,16,256]{2,1,0:T(8,128)(2,1)S(1)} all-to-all(bf16[32,16,256]{2,1,0:T(8,128)(2,1)S(1)} %maximum_maximum_fusion), channel_id=1, replica_groups=mesh['y'=4,'z'=8,'c'=2,'x'=4] {'y','z'}, dimensions={0} | all-to-all | bytes 524288 | tf_op jit(solution)/shard_map/dv_yz/all_to_all | solution.py:271
  127.7 0.7 broadcast_in_dim.24
  128.4 6.3 %all-to-all-start.3 = ((bf16[32,16,256]{2,1,0:T(8,128)(2,1)}), bf16[32,16,256]{2,1,0:T(8,128)(2,1)S(1)}, u32[]{:S(2)}, u32[]{:S(2)}) async-start(bf16[32,16,256]{2,1,0:T(8,128)(2,1)} %broadcast_in_dim.24), calls=%async_computation.5 | async-start | bytes 524288 | tf_op jit(solution)/shard_map/all_yz/all_to_all | solution.py:271
  134.7 0.7 reduce-scatter.5.cloned.1.call-update
  135.4 8.9 %all-to-all-done.3 = bf16[32,16,256]{2,1,0:T(8,128)(2,1)S(1)} async-done(((bf16[32,16,256]{2,1,0:T(8,128)(2,1)}), bf16[32,16,256]{2,1,0:T(8,128)(2,1)S(1)}, u32[]{:S(2)}, u32[]{:S(2)}) %all-to-all-start.3) | async-done | bytes 262176 | tf_op jit(solution)/shard_map/all_yz/all_to_all | solution.py:271
  144.4 9.4 %all_to_all.27 = bf16[4,256,256]{2,1,0:T(8,128)(2,1)S(1)} all-to-all(bf16[4,256,256]{2,1,0:T(8,128)(2,1)S(1)} %broadcast_in_dim.52), channel_id=1, replica_groups=mesh['y'=4,'z'=8,'c'=2,'x'=4] {'x'}, dimensions={0} | all-to-all | bytes 1048576 | tf_op jit(solution)/shard_map/all_x/all_to_all | solution.py:271
  153.8 5.1 %collective-permute-start.3 = (bf16[1024,256]{1,0:T(8,128)(2,1)S(1)}, bf16[1024,256]{1,0:T(8,128)(2,1)S(1)}, u32[]{:S(2)}, u32[]{:S(2)}) collective-permute-start(bf16[1024,256]{1,0:T(8,128)(2,1)S(1)} %bitcast.30), channel_id=1, source_target_pairs={{0,4},{4,0},{1,5},{5,1},{2,6},{6,2},{3,7},{7,3},{8,12},{12,8},{9,1... | collective-permute-start | bytes 1572872 | tf_op jit(solution)/shard_map/all_c/ppermute | solution.py:267
  159.8 0.7 copy.31
  160.5 0.8 reduce-scatter.5.cloned.1.call-done
  161.3 2.0 %fusion.1 = f32[256,256]{1,0:T(8,128)} fusion(f32[128,256]{1,0:T(8,128)} %reduce-scatter.5.cloned.1.call-done, f32[128]{0:T(128)S(1)} %convert_reduce_fusion.2, s32[256]{0:T(256)S(1)} %copy-done.7), kind=kOutput, calls=%fused_computation.13 | convolution fusion | flops 100728832 | bytes 394752 | tf_op jit(solution)/shard_map/dot_general | solution.py:380
  163.4 1.5 convert_multiply_fusion
  (51 shorter events, 3.4 us)
Async XLA Ops:
  8.0 0.9 copy-start
  8.0 28.9 %copy-start.3 = (bf16[128,256]{1,0:T(8,128)(2,1)S(1)}, bf16[128,256]{1,0:T(8,128)(2,1)}, u32[]{:S(2)}) copy-start(bf16[128,256]{1,0:T(8,128)(2,1)} %param.19) | copy-start | bytes 196612
  8.0 27.6 %copy-start.4 = (s32[32]{0:T(128)S(1)}, s32[32]{0:T(128)}, u32[]{:S(2)}) copy-start(s32[32]{0:T(128)} %param.15) | copy-start | bytes 388
  8.0 27.6 %copy-start.5 = (s32[32]{0:T(128)S(1)}, s32[32]{0:T(128)}, u32[]{:S(2)}) copy-start(s32[32]{0:T(128)} %param.14) | copy-start | bytes 388
  8.0 28.1 %copy-start.6 = (bf16[500,8]{0,1:T(8,128)(2,1)S(1)}, bf16[500,8]{0,1:T(8,128)(2,1)}, u32[]{:S(2)}) copy-start(bf16[500,8]{0,1:T(8,128)(2,1)} %param.17) | copy-start | bytes 24004
  8.1 59.7 %all-gather.2.cloned.1.call-start = ((), (), s32[]{:S(2)}) async-start(), calls=%async_computation.7 | async-start | bytes 2621440 | tf_op jit(solution)/shard_map/feats_y/all_gather | solution.py:321
  34.9 92.8 %reduce-scatter.3.cloned.1.call-start = ((), (), s32[]{:S(2)}) async-start(), calls=%async_computation.8 | async-start | bytes 4718592 | tf_op jit(solution)/shard_map/dx_z/reduce_scatter | solution.py:332
  53.5 9.9 %collective-permute-start.2 = (bf16[32,128,256]{2,1,0:T(8,128)(2,1)}, bf16[32,128,256]{2,1,0:T(8,128)(2,1)S(1)}, u32[]{:S(2)}, u32[]{:S(2)}) collective-permute-start(bf16[32,128,256]{2,1,0:T(8,128)(2,1)} %get-tuple-element.23), channel_id=1, source_target_pairs={{0,4},{4,0},{1,5},{5,1},{2,6},{6,2},{3,7},{7,3},{8,12},{12,8},{9,1... | collective-permute-start | bytes 6291464 | tf_op jit(solution)/shard_map/dx_c/ppermute | solution.py:267
  67.7 4.5 %collective-permute-start = (bf16[32,128,256]{2,1,0:T(8,128)(2,1)}, bf16[32,128,256]{2,1,0:T(8,128)(2,1)S(1)}, u32[]{:S(2)}, u32[]{:S(2)}) collective-permute-start(bf16[32,128,256]{2,1,0:T(8,128)(2,1)} %bitcast.28), channel_id=1, source_target_pairs={{0,4},{4,0},{1,5},{5,1},{2,6},{6,2},{3,7},{7,3},{8,12},{12,8},{9,1... | collective-permute-start | bytes 6291464 | tf_op jit(solution)/shard_map/feats_c/ppermute | solution.py:267
  72.2 1.3 copy-start.1
  82.3 4.7 %copy-start.2 = (bf16[512,256]{1,0:T(8,128)(2,1)S(1)}, bf16[512,256]{1,0:T(8,128)(2,1)}, u32[]{:S(2)}) copy-start(bf16[512,256]{1,0:T(8,128)(2,1)} %get-tuple-element.20) | copy-start | bytes 786436
  82.4 2.5 %collective-permute-start.1 = (bf16[1056,256]{1,0:T(8,128)(2,1)}, bf16[1056,256]{1,0:T(8,128)(2,1)S(1)}, u32[]{:S(2)}, u32[]{:S(2)}) collective-permute-start(bf16[1056,256]{1,0:T(8,128)(2,1)} %get-tuple-element.19), channel_id=1, source_target_pairs={{0,4},{4,0},{1,5},{5,1},{2,6},{6,2},{3,7},{7,3},{8,12},{12,8},{9,1... | collective-permute-start | bytes 1622024 | tf_op jit(solution)/shard_map/dv_c/ppermute | solution.py:267
  88.0 20.3 %all-to-all-start.1 = ((bf16[4,416,256]{2,1,0:T(8,128)(2,1)}), bf16[4,416,256]{2,1,0:T(8,128)(2,1)S(1)}, u32[]{:S(2)}, u32[]{:S(2)}) async-start(bf16[4,416,256]{2,1,0:T(8,128)(2,1)} %pad_maximum_fusion), calls=%async_computation.1 | async-start | bytes 1703936 | tf_op jit(solution)/shard_map/dv_x/all_to_all | solution.py:271
  128.4 32.9 %copy-start.7 = (s32[256]{0:T(256)S(1)}, s32[256]{0:T(256)}, u32[]{:S(2)}) copy-start(s32[256]{0:T(256)} %param.11) | copy-start | bytes 3076
  128.4 16.0 %all-to-all-start.3 = ((bf16[32,16,256]{2,1,0:T(8,128)(2,1)}), bf16[32,16,256]{2,1,0:T(8,128)(2,1)S(1)}, u32[]{:S(2)}, u32[]{:S(2)}) async-start(bf16[32,16,256]{2,1,0:T(8,128)(2,1)} %broadcast_in_dim.24), calls=%async_computation.5 | async-start | bytes 524288 | tf_op jit(solution)/shard_map/all_yz/all_to_all | solution.py:271
  134.7 26.6 %reduce-scatter.5.cloned.1.call-start = ((), (), s32[]{:S(2)}) async-start(), calls=%async_computation.9 | async-start | bytes 655360 | tf_op jit(solution)/shard_map/dx_y/reduce_scatter | solution.py:365
  153.8 9.4 %collective-permute-start.3 = (bf16[1024,256]{1,0:T(8,128)(2,1)S(1)}, bf16[1024,256]{1,0:T(8,128)(2,1)S(1)}, u32[]{:S(2)}, u32[]{:S(2)}) collective-permute-start(bf16[1024,256]{1,0:T(8,128)(2,1)S(1)} %bitcast.30), channel_id=1, source_target_pairs={{0,4},{4,0},{1,5},{5,1},{2,6},{6,2},{3,7},{7,3},{8,12},{12,8},{9,1... | collective-permute-start | bytes 1572872 | tf_op jit(solution)/shard_map/all_c/ppermute | solution.py:267
Sparse Core Ops, SparseCore 0:
  35.0 31.5 all-gather.1
  138.1 23.2 reduce-scatter.4
Sparse Core Ops, SparseCore 1:
  67.8 52.9 reduce-scatter.2

commit v3 on v2

--- a/solution.py
+++ b/solution.py
@@ -310,15 +310,15 @@
     other = (tile_column_index % 2 != mine).astype(jnp.int32) * SLOTS
     ty = tile_column_index // (2 * NZ)
     tz = (tile_column_index // 2) % NZ
-    xslot = other + ty * NZ + tz
-    dslot = other + tz * NY + ty
+    xslot = other + tz * NY + ty
+    dslot = other + ty * NZ + tz
     stacked = bases.reshape(B * H, H)
 
+    with jax.named_scope("feats_y"):
+        feats_y = spread_to(class_feat, "y", NY).reshape(NY * TILE, H)
+    cotangent, feats_y = after(cotangent, feats_y)
     with jax.named_scope("feats_z"):
-        feats_z = spread_to(class_feat, "z", NZ).reshape(NZ * TILE, H)
-    cotangent, feats_z = after(cotangent, feats_z)
-    with jax.named_scope("feats_y"):
-        feats_mine = lax.all_gather(feats_z, "y", axis=0, tiled=True)
+        feats_mine = lax.all_gather(feats_y, "z", axis=0, tiled=True)
     with jax.named_scope("cot_x"):
         cot_rows = lax.all_gather(cotangent, "x", axis=0, tiled=True)
 
@@ -327,9 +327,10 @@
     )
     with jax.named_scope("dx_c"):
         got = swap(give)
-    dx = (keep.astype(F32) + got.astype(F32)).reshape(NZ * NY * TILE, H)
-    with jax.named_scope("dx_z"):
-        dx = lax.psum_scatter(dx, "z", scatter_dimension=0, tiled=True)
+    dx = (keep.astype(F32) + got.astype(F32)).astype(BF16).reshape(NY * NZ * TILE, H)
+    with jax.named_scope("dx_y"):
+        dx = lax.psum_scatter(dx, "y", scatter_dimension=0, tiled=True)
+
     feats_mine = feats_mine.reshape(SLOTS, TILE, H)
     with jax.named_scope("feats_c"):
         feats_other = swap(feats_mine)
@@ -346,6 +347,9 @@
     cg_x = jnp.broadcast_to(two_parts(cg)[None], (NX, 32, H))
     with jax.named_scope("dv_x"):
         got_x = exchange(jnp.concatenate([dv, outp.reshape(NX, TILE, H), cg_x], axis=1), "x")
+    got_x, dx = after(got_x, dx)
+    with jax.named_scope("dx_z"):
+        dx = lax.psum_scatter(dx.astype(F32), "z", scatter_dimension=0, tiled=True)
     sum_x = jnp.sum(got_x.astype(F32), axis=0)
     layer_out = sum_x[256:384].astype(BF16)
     cg = sum_x[384:, :128] + sum_x[384:, 128:]
@@ -360,9 +364,6 @@
     packed = jnp.concatenate(
         [sum_yz[:8].astype(BF16), two_parts(cg), jnp.zeros((7, H), BF16)], axis=0
     )
-    packed, dx = after(packed, dx)
-    with jax.named_scope("dx_y"):
-        dx = lax.psum_scatter(dx, "y", scatter_dimension=0, tiled=True)
     with jax.named_scope("all_yz"):
         all_yz = spread_to(packed, ("y", "z"), NY * NZ)
     scale = (NY * NZ * NC * NX * TILE) ** (-0.5)
@@ -370,6 +371,7 @@
     grad_coef = (cg * scale).reshape(512, B)[:RELS]
     with jax.named_scope("all_x"):
         all_x = spread_to(all_yz[:, :8].reshape(256, H), "x", NX).reshape(1024, H)
+    all_x, dx = after(all_x, dx)
     with jax.named_scope("all_c"):
         all_other = swap(all_x)
     first = jnp.where(mine == 0, all_x, all_other)

time: 174 us -> 173 us (level)
  blocking collectives: 63.7 us -> 48.9 us
  waiting for transfers between devices: 30.8 us -> 39.6 us
  Pallas kernels: 14.9 us -> 19.3 us
  other arithmetic: 11.2 us -> 13.1 us
    all_to_all x3, blocking collectives: 53.3 us -> 36.5 us  [exchange(): return lax.all_to_all(x, axes, split_axis=0, concat_axis=0, tiled=True)]
    reduce_scatter x1, waiting for transfers between devices: 0.01 us -> 5.91 us  [local(): dx = lax.psum_scatter(dx.astype(F32), 'z', scatter_dimension=0, tiled=True)]
    convert_element_type x0 -> x2, other arithmetic: none -> 4.71 us  [the longest x1 3.67 us: local(): (keep.astype(F32) + got.astype(F32)).astype(BF16).reshape(NY * NZ * TILE, H)]
    all_gather x1, waiting for transfers between devices: 0.02 us -> 4.69 us  [local(): feats_mine = lax.all_gather(feats_y, 'z', axis=0, tiled=True)]
    add x3 -> x2, other arithmetic: 5.29 us -> 1.77 us  [the longest x1 1.18 us: local(): dslot = other + ty * NZ + tz]
    pallas_call x1, Pallas kernels: 8.82 us -> 11.4 us  [forward(): pl.pallas_call(forward_kernel, in_specs=[SMEM] * 5 + [VMEM] * 2 + [ANY] *...]
    all_gather x1, blocking collectives: 10.4 us -> 12.3 us  [local(): cot_rows = lax.all_gather(cotangent, 'x', axis=0, tiled=True)]
    pallas_call x1, Pallas kernels: 6.11 us -> 7.92 us  [backward(): pl.pallas_call(backward_kernel, in_specs=[SMEM] * 4 + [ANY] * 3, out_spec...]
  transfers between devices with their start and end apart: 9 -> 9, of which waited for: 6 -> 7; matrix products, arithmetic and copies ran while one was open for 9% -> 10% of each run, Pallas kernels for 9% -> 11%
where the time goes in v3:
time: 173 us; the launch traced here: 172 us
  blocking collectives  48.9 us (28%)
  waiting for transfers between devices  39.6 us (23%)
  starting transfers between devices  25.1 us (15%)
  Pallas kernels  19.3 us (11%)
  between operations  16.3 us (9%)
  other arithmetic  13.1 us (8%)
  local copies, waits for them, and re-layouts  5.21 us (3%)
  matrix products  4.41 us (3%)
    all_to_all x3, blocking collectives, exchange(): return lax.all_to_all(x, axes, split_axis=0, concat_axis=0, tiled=True)  36.5 us
    all_to_all x2, waiting for transfers between devices, exchange(): return lax.all_to_all(x, axes, split_axis=0, concat_axis=0, tiled=True)  20.9 us
    all_to_all x2, starting transfers between devices, exchange(): return lax.all_to_all(x, axes, split_axis=0, concat_axis=0, tiled=True)  13.6 us
    all_gather x1, blocking collectives, local(): cot_rows = lax.all_gather(cotangent, 'x', axis=0, tiled=True)  12.3 us
    pallas_call x1, Pallas kernels, forward(): pl.pallas_call(forward_kernel, in_specs=[SMEM] * 5 + [VMEM] * 2 + [ANY] *...  11.4 us
    ppermute x4, starting transfers between devices, swap(): return lax.ppermute(x, 'c', [(0, 1), (1, 0)])  11.3 us
    ppermute x4, waiting for transfers between devices, swap(): return lax.ppermute(x, 'c', [(0, 1), (1, 0)])  8.09 us
    pallas_call x1, Pallas kernels, backward(): pl.pallas_call(backward_kernel, in_specs=[SMEM] * 4 + [ANY] * 3, out_spec...  7.92 us
  transfers between devices with their start and end apart: 9, of which 7 were waited for; matrix products, arithmetic and copies ran while one was open for 10% of the time, Pallas kernels for 11%

profile of v3, /device:TPU:1, one launch (start us, length us, event | category | flops | bytes accessed | tf_op | source)
XLA Modules:
  0.0 171.9 jit_solution(18392510140544682831)
XLA Ops:
  8.1 0.8 convert_reduce_fusion.2
  8.9 1.0 fusion
  9.9 10.4 %all_to_all.25 = bf16[4,128,256]{2,1,0:T(8,128)(2,1)} all-to-all(bf16[4,128,256]{2,1,0:T(8,128)(2,1)S(1)} %broadcast_in_dim.20), channel_id=1, replica_groups=mesh['y'=4,'z'=8,'c'=2,'x'=4] {'y'}, dimensions={0} | all-to-all | bytes 524288 | tf_op jit(solution)/shard_map/feats_y/all_to_all | solution.py:271
  21.7 1.2 add_add_fusion
  22.9 1.5 fusion.3.coef
  24.4 12.3 %all_gather.7.cot_in = bf16[512,256]{1,0:T(8,128)(2,1)} all-gather(bf16[128,256]{1,0:T(8,128)(2,1)} %param.19), channel_id=1, replica_groups=mesh['y'=4,'z'=8,'c'=2,'x'=4] {'x'}, dimensions={0}, use_global_device_ids=true | all-gather | bytes 327680 | tf_op jit(solution)/shard_map/cot_x/all_gather | solution.py:323
  36.8 7.9 %backward.1 = (bf16[4,8,128,256]{3,2,1,0:T(8,128)(2,1)}, bf16[32,128,256]{2,1,0:T(8,128)(2,1)}, bf16[32,128,256]{2,1,0:T(8,128)(2,1)}) custom-call(s32[32]{0:T(128)} %trow.3, s32[32]{0:T(128)} %get-tuple-element.42.dslot, s32[1]{0:T(128)S(6)} %copy.33.count, f32[40,8]{1,0:T(8,128)} %fusion.3.coef, bf16[512,256]{1,0:T(8,128)(2,1)} %all_gather.7.cot_in, ...), custom_call_target="tpu_custom_call" | custom-call | tf_op jit(solution)/shard_map/backward/pallas_call | solution.py:128
  44.7 3.3 %collective-permute-start.2 = (bf16[32,128,256]{2,1,0:T(8,128)(2,1)}, bf16[32,128,256]{2,1,0:T(8,128)(2,1)S(1)}, u32[]{:S(2)}, u32[]{:S(2)}) collective-permute-start(bf16[32,128,256]{2,1,0:T(8,128)(2,1)} %get-tuple-element.25), channel_id=1, source_target_pairs={{0,4},{4,0},{1,5},{5,1},{2,6},{6,2},{3,7},{7,3},{8,12},{12,8},{9,1... | collective-permute-start | bytes 6291464 | tf_op jit(solution)/shard_map/dx_c/ppermute | solution.py:267
  48.0 4.0 %collective-permute-done.2 = bf16[32,128,256]{2,1,0:T(8,128)(2,1)S(1)} collective-permute-done((bf16[32,128,256]{2,1,0:T(8,128)(2,1)}, bf16[32,128,256]{2,1,0:T(8,128)(2,1)S(1)}, u32[]{:S(2)}, u32[]{:S(2)}) %collective-permute-start.2) | collective-permute-done | bytes 2097184 | tf_op jit(solution)/shard_map/dx_c/ppermute | solution.py:267
  52.0 3.7 %add_convert_fusion = bf16[32,128,256]{2,1,0:T(8,128)(2,1)} fusion(bf16[32,128,256]{2,1,0:T(8,128)(2,1)S(1)} %collective-permute-done.2, bf16[32,128,256]{2,1,0:T(8,128)(2,1)} %get-tuple-element.24), kind=kLoop, calls=%fused_computation | loop fusion | flops 4194304 | bytes 6291456 | tf_op jit(solution)/shard_map/convert_element_type | solution.py:330
  55.7 4.7 %all-gather.2.cloned.1.call-done = bf16[4096,256]{1,0:T(8,128)(2,1)} async-done(((bf16[512,256]{1,0:T(8,128)(2,1)}), bf16[4096,256]{1,0:T(8,128)(2,1)}) %all-gather.2.cloned.1.call-update) | async-done | bytes 2097168 | tf_op jit(solution)/shard_map/feats_z/all_gather | solution.py:321
  60.4 4.3 %collective-permute-start = (bf16[32,128,256]{2,1,0:T(8,128)(2,1)}, bf16[32,128,256]{2,1,0:T(8,128)(2,1)S(1)}, u32[]{:S(2)}, u32[]{:S(2)}) collective-permute-start(bf16[32,128,256]{2,1,0:T(8,128)(2,1)} %bitcast.26), channel_id=1, source_target_pairs={{0,4},{4,0},{1,5},{5,1},{2,6},{6,2},{3,7},{7,3},{8,12},{12,8},{9,1... | collective-permute-start | bytes 6291464 | tf_op jit(solution)/shard_map/feats_c/ppermute | solution.py:267
  64.8 0.8 broadcast_in_dim_reshape.8.relc
  66.7 2.0 %collective-permute-done.xother = bf16[32,128,256]{2,1,0:T(8,128)(2,1)S(1)} collective-permute-done((bf16[32,128,256]{2,1,0:T(8,128)(2,1)}, bf16[32,128,256]{2,1,0:T(8,128)(2,1)S(1)}, u32[]{:S(2)}, u32[]{:S(2)}) %collective-permute-start) | collective-permute-done | bytes 2097184 | tf_op jit(solution)/shard_map/feats_c/ppermute | solution.py:267
  68.7 1.3 copy-done.1
  70.0 11.4 %forward.1 = (bf16[512,256]{1,0:T(8,128)(2,1)}, f32[1024,256]{1,0:T(8,128)}, bf16[1056,256]{1,0:T(8,128)(2,1)}, f32[32,128]{1,0:T(8,128)}) custom-call(s32[32]{0:T(128)} %trow.3, s32[32]{0:T(128)} %add_add_fusion.1.xslot, s32[1]{0:T(128)S(6)} %copy.33.count, s32[1]{0:T(128)} %bitcast.half, f32[40,8]{1,0:T(8,128)} %fusion.3.coef, ...), custom_call_target="tpu_custom_call" | custom-call | tf_op jit(solution)/shard_map/forward/pallas_call | solution.py:237
  81.5 2.1 %collective-permute-done.1 = bf16[1056,256]{1,0:T(8,128)(2,1)S(1)} collective-permute-done((bf16[1056,256]{1,0:T(8,128)(2,1)}, bf16[1056,256]{1,0:T(8,128)(2,1)S(1)}, u32[]{:S(2)}, u32[]{:S(2)}) %collective-permute-start.1) | collective-permute-done | bytes 540704 | tf_op jit(solution)/shard_map/dv_c/ppermute | solution.py:267
  83.6 0.7 reduce-precision_convert_fusion.1
  84.4 1.4 add_convert_fusion.1
  85.8 1.0 pad_maximum_fusion
  86.7 3.6 %all-to-all-start.1 = ((bf16[4,416,256]{2,1,0:T(8,128)(2,1)}), bf16[4,416,256]{2,1,0:T(8,128)(2,1)S(1)}, u32[]{:S(2)}, u32[]{:S(2)}) async-start(bf16[4,416,256]{2,1,0:T(8,128)(2,1)} %pad_maximum_fusion), calls=%async_computation.1 | async-start | bytes 1703936 | tf_op jit(solution)/shard_map/dv_x/all_to_all | solution.py:271
  90.4 12.4 %all-to-all-done.1 = bf16[4,416,256]{2,1,0:T(8,128)(2,1)S(1)} async-done(((bf16[4,416,256]{2,1,0:T(8,128)(2,1)}), bf16[4,416,256]{2,1,0:T(8,128)(2,1)S(1)}, u32[]{:S(2)}, u32[]{:S(2)}) %all-to-all-start.1) | async-done | bytes 852000 | tf_op jit(solution)/shard_map/dv_x/all_to_all | solution.py:271
  103.0 0.8 maximum_maximum_fusion
  103.8 10.0 %all-to-all-start.2 = ((bf16[32,16,256]{2,1,0:T(8,128)(2,1)}), bf16[32,16,256]{2,1,0:T(8,128)(2,1)S(1)}, u32[]{:S(2)}, u32[]{:S(2)}) async-start(bf16[32,16,256]{2,1,0:T(8,128)(2,1)} %maximum_maximum_fusion), calls=%async_computation.3 | async-start | bytes 524288 | tf_op jit(solution)/shard_map/dv_yz/all_to_all | solution.py:271
  113.9 1.0 convert_element_type.99
  115.0 8.5 %all-to-all-done.2 = bf16[32,16,256]{2,1,0:T(8,128)(2,1)S(1)} async-done(((bf16[32,16,256]{2,1,0:T(8,128)(2,1)}), bf16[32,16,256]{2,1,0:T(8,128)(2,1)S(1)}, u32[]{:S(2)}, u32[]{:S(2)}) %all-to-all-start.2) | async-done | bytes 262176 | tf_op jit(solution)/shard_map/dv_yz/all_to_all | solution.py:271
  123.7 16.8 %all_to_all.26 = bf16[32,16,256]{2,1,0:T(8,128)(2,1)S(1)} all-to-all(bf16[32,16,256]{2,1,0:T(8,128)(2,1)S(1)} %broadcast_in_dim.24), channel_id=1, replica_groups=mesh['y'=4,'z'=8,'c'=2,'x'=4] {'y','z'}, dimensions={0} | all-to-all | bytes 524288 | tf_op jit(solution)/shard_map/all_yz/all_to_all | solution.py:271
  140.5 9.3 %all_to_all.27 = bf16[4,256,256]{2,1,0:T(8,128)(2,1)S(1)} all-to-all(bf16[4,256,256]{2,1,0:T(8,128)(2,1)S(1)} %broadcast_in_dim.52), channel_id=1, replica_groups=mesh['y'=4,'z'=8,'c'=2,'x'=4] {'x'}, dimensions={0} | all-to-all | bytes 1048576 | tf_op jit(solution)/shard_map/all_x/all_to_all | solution.py:271
  149.8 5.9 %reduce-scatter.5.cloned.1.call-done = f32[128,256]{1,0:T(8,128)} async-done(((f32[1024,256]{1,0:T(8,128)}), f32[128,256]{1,0:T(8,128)}) %reduce-scatter.5.cloned.1.call-update) | async-done | bytes 131088 | tf_op jit(solution)/shard_map/dx_z/reduce_scatter | solution.py:352
  155.7 3.6 %collective-permute-start.3 = (bf16[1024,256]{1,0:T(8,128)(2,1)S(1)}, bf16[1024,256]{1,0:T(8,128)(2,1)S(1)}, u32[]{:S(2)}, u32[]{:S(2)}) collective-permute-start(bf16[1024,256]{1,0:T(8,128)(2,1)S(1)} %bitcast.28), channel_id=1, source_target_pairs={{0,4},{4,0},{1,5},{5,1},{2,6},{6,2},{3,7},{7,3},{8,12},{12,8},{9,1... | collective-permute-start | bytes 1572872 | tf_op jit(solution)/shard_map/all_c/ppermute | solution.py:267
  160.9 2.0 %fusion.1 = f32[256,256]{1,0:T(8,128)} fusion(f32[128,256]{1,0:T(8,128)} %reduce-scatter.5.cloned.1.call-done, f32[128]{0:T(128)S(1)} %convert_reduce_fusion.2, s32[256]{0:T(256)S(1)} %copy-done.5), kind=kOutput, calls=%fused_computation.13 | convolution fusion | flops 100728832 | bytes 394752 | tf_op jit(solution)/shard_map/dot_general | solution.py:382
  163.0 1.5 convert_multiply_fusion
  (48 shorter events, 4.4 us)
Async XLA Ops:
  8.0 0.9 copy-start
  8.0 52.3 %all-gather.2.cloned.1.call-start = ((), (), s32[]{:S(2)}) async-start(), calls=%async_computation.7 | async-start | bytes 2359296 | tf_op jit(solution)/shard_map/feats_z/all_gather | solution.py:321
  20.4 70.1 %reduce-scatter.3.cloned.1.call-start = ((), (), s32[]{:S(2)}) async-start(), calls=%async_computation.8 | async-start | bytes 2621440 | tf_op jit(solution)/shard_map/dx_y/reduce_scatter | solution.py:332
  44.7 7.3 %collective-permute-start.2 = (bf16[32,128,256]{2,1,0:T(8,128)(2,1)}, bf16[32,128,256]{2,1,0:T(8,128)(2,1)S(1)}, u32[]{:S(2)}, u32[]{:S(2)}) collective-permute-start(bf16[32,128,256]{2,1,0:T(8,128)(2,1)} %get-tuple-element.25), channel_id=1, source_target_pairs={{0,4},{4,0},{1,5},{5,1},{2,6},{6,2},{3,7},{7,3},{8,12},{12,8},{9,1... | collective-permute-start | bytes 6291464 | tf_op jit(solution)/shard_map/dx_c/ppermute | solution.py:267
  55.6 9.1 %copy-start.4 = (s32[32]{0:T(128)S(1)}, s32[32]{0:T(128)}, u32[]{:S(2)}) copy-start(s32[32]{0:T(128)} %param.15) | copy-start | bytes 388
  60.4 8.3 %collective-permute-start = (bf16[32,128,256]{2,1,0:T(8,128)(2,1)}, bf16[32,128,256]{2,1,0:T(8,128)(2,1)S(1)}, u32[]{:S(2)}, u32[]{:S(2)}) collective-permute-start(bf16[32,128,256]{2,1,0:T(8,128)(2,1)} %bitcast.26), channel_id=1, source_target_pairs={{0,4},{4,0},{1,5},{5,1},{2,6},{6,2},{3,7},{7,3},{8,12},{12,8},{9,1... | collective-permute-start | bytes 6291464 | tf_op jit(solution)/shard_map/feats_c/ppermute | solution.py:267
  68.7 1.3 copy-start.1
  81.4 4.4 %copy-start.3 = (bf16[512,256]{1,0:T(8,128)(2,1)S(1)}, bf16[512,256]{1,0:T(8,128)(2,1)}, u32[]{:S(2)}) copy-start(bf16[512,256]{1,0:T(8,128)(2,1)} %get-tuple-element.22) | copy-start | bytes 786436
  81.4 2.2 %collective-permute-start.1 = (bf16[1056,256]{1,0:T(8,128)(2,1)}, bf16[1056,256]{1,0:T(8,128)(2,1)S(1)}, u32[]{:S(2)}, u32[]{:S(2)}) collective-permute-start(bf16[1056,256]{1,0:T(8,128)(2,1)} %get-tuple-element.21), channel_id=1, source_target_pairs={{0,4},{4,0},{1,5},{5,1},{2,6},{6,2},{3,7},{7,3},{8,12},{12,8},{9,1... | collective-permute-start | bytes 1622024 | tf_op jit(solution)/shard_map/dv_c/ppermute | solution.py:267
  86.7 16.1 %all-to-all-start.1 = ((bf16[4,416,256]{2,1,0:T(8,128)(2,1)}), bf16[4,416,256]{2,1,0:T(8,128)(2,1)S(1)}, u32[]{:S(2)}, u32[]{:S(2)}) async-start(bf16[4,416,256]{2,1,0:T(8,128)(2,1)} %pad_maximum_fusion), calls=%async_computation.1 | async-start | bytes 1703936 | tf_op jit(solution)/shard_map/dv_x/all_to_all | solution.py:271
  90.4 23.5 %copy-start.2 = (bf16[1024,256]{1,0:T(8,128)(2,1)S(1)}, bf16[1024,256]{1,0:T(8,128)(2,1)}, u32[]{:S(2)}) copy-start(bf16[1024,256]{1,0:T(8,128)(2,1)} %reduce-scatter.3.cloned.1.call-done) | copy-start | bytes 1572868
  103.8 19.7 %all-to-all-start.2 = ((bf16[32,16,256]{2,1,0:T(8,128)(2,1)}), bf16[32,16,256]{2,1,0:T(8,128)(2,1)S(1)}, u32[]{:S(2)}, u32[]{:S(2)}) async-start(bf16[32,16,256]{2,1,0:T(8,128)(2,1)} %maximum_maximum_fusion), calls=%async_computation.3 | async-start | bytes 524288 | tf_op jit(solution)/shard_map/dv_yz/all_to_all | solution.py:271
  113.8 41.9 %reduce-scatter.5.cloned.1.call-start = ((), (), s32[]{:S(2)}) async-start(), calls=%async_computation.9 | async-start | bytes 1179648 | tf_op jit(solution)/shard_map/dx_z/reduce_scatter | solution.py:352
  115.0 46.0 %copy-start.5 = (s32[256]{0:T(256)S(1)}, s32[256]{0:T(256)}, u32[]{:S(2)}) copy-start(s32[256]{0:T(256)} %param.11) | copy-start | bytes 3076
  155.7 7.1 %collective-permute-start.3 = (bf16[1024,256]{1,0:T(8,128)(2,1)S(1)}, bf16[1024,256]{1,0:T(8,128)(2,1)S(1)}, u32[]{:S(2)}, u32[]{:S(2)}) collective-permute-start(bf16[1024,256]{1,0:T(8,128)(2,1)S(1)} %bitcast.28), channel_id=1, source_target_pairs={{0,4},{4,0},{1,5},{5,1},{2,6},{6,2},{3,7},{7,3},{8,12},{12,8},{9,1... | collective-permute-start | bytes 1572872 | tf_op jit(solution)/shard_map/all_c/ppermute | solution.py:267
Sparse Core Ops, SparseCore 0:
  20.5 39.8 all-gather.1
  118.0 37.7 reduce-scatter.4
Sparse Core Ops, SparseCore 1:
  55.7 33.3 reduce-scatter.2

commit v4 on v3

--- a/solution.py
+++ b/solution.py
@@ -19,7 +19,15 @@
 VMEM = pl.BlockSpec(memory_space=pltpu.VMEM)
 SMEM = pl.BlockSpec(memory_space=pltpu.SMEM)
 ANY = pl.BlockSpec(memory_space=pl.ANY)
-PARAMS = pltpu.CompilerParams(vmem_limit_bytes=56 * 2**20)
+PARAMS = pltpu.CompilerParams(vmem_limit_bytes=32 * 2**20)
+
+
+def far(x):
+    return pltpu.with_memory_space_constraint(x, pltpu.HBM)
+
+
+def near(x):
+    return pltpu.with_memory_space_constraint(x, pltpu.VMEM)
 
 
 def by_row(trow, count, order, filled):
@@ -64,27 +72,19 @@
 
 
 def backward_kernel(
-    trow, dslot, count, coef, cot_in, bases_in, tiles_in, grads_out, keep_out, give_out,
-    cot, bases, tiles, wide, grads, total, mixed, narrow, order, filled, sems,
+    trow, dslot, count, coef, cot, bases, tiles, grads_out, keep, give,
+    grads, wide, total, mixed, order, filled, sem,
 ):
-    loads = [
-        pltpu.make_async_copy(src, dst, sems.at[k])
-        for k, (src, dst) in enumerate(((cot_in, cot), (bases_in, bases), (tiles_in, tiles)))
-    ]
-    for copy in loads:
-        copy.start()
     total[...] = jnp.zeros_like(total)
     mixed[...] = jnp.zeros_like(mixed)
     by_row(trow, count, order, filled)
-    loads[0].wait()
-    loads[1].wait()
     for b in range(B):
         g = lax.dot_general(
             cot[...], bases[pl.ds(b * H, H), :], (((1,), (1,)), ((), ())), preferred_element_type=F32
         ).astype(BF16)
         grads[:, b] = g.reshape(TROWS, TILE, H)
         wide[:, b] = g.astype(F32).reshape(TROWS, TILE, H)
-    store = pltpu.make_async_copy(grads, grads_out, sems.at[3])
+    store = pltpu.make_async_copy(grads, grads_out, sem)
     store.start()
 
     def mix(t, s1, s2):
@@ -103,7 +103,6 @@
             mixed[s2, rows, :] = m2.astype(BF16)
 
     pairs(order, filled, mix)
-    loads[2].wait()
 
     def back(s):
         d = dslot[s]
@@ -112,57 +111,46 @@
         )
 
     fours(count, back)
-    outs = []
-    for k, out in ((1, give_out), (0, keep_out)):
-        narrow[k] = total[pl.ds(k * SLOTS, SLOTS)].astype(BF16)
-        copy = pltpu.make_async_copy(narrow.at[k], out, sems.at[4 + k])
-        copy.start()
-        outs.append(copy)
+    keep[...] = total[pl.ds(0, SLOTS)].astype(BF16)
+    give[...] = total[pl.ds(SLOTS, SLOTS)].astype(BF16)
     store.wait()
-    for copy in outs:
-        copy.wait()
 
 
 def backward(trow, dslot, count, coef, cot_rows, stacked, tile_values):
-    blocks = jax.ShapeDtypeStruct((SLOTS, TILE, H), BF16)
+    blocks = pltpu.VMEM((SLOTS, TILE, H), BF16)
     return pl.pallas_call(
         backward_kernel,
-        in_specs=[SMEM] * 4 + [ANY] * 3,
-        out_specs=[ANY] * 3,
-        out_shape=[jax.ShapeDtypeStruct((TROWS, B, TILE, H), BF16), blocks, blocks],
+        in_specs=[SMEM] * 4 + [VMEM] * 3,
+        out_specs=[ANY] + [VMEM] * 2,
+        out_shape=[pltpu.HBM((TROWS, B, TILE, H), BF16), blocks, blocks],
         scratch_shapes=[
-            pltpu.VMEM((TROWS * TILE, H), BF16),
-            pltpu.VMEM((B * H, H), BF16),
-            pltpu.VMEM((SLOTS, TILE, TILE), BF16),
+            pltpu.VMEM((TROWS, B, TILE, H), BF16),
             pltpu.VMEM((TROWS, B, TILE, H), F32),
-            pltpu.VMEM((TROWS, B, TILE, H), BF16),
             pltpu.VMEM((2 * SLOTS, TILE, H), F32),
             pltpu.VMEM((SLOTS + 1, TILE, H), BF16),
-            pltpu.VMEM((2, SLOTS, TILE, H), BF16),
             pltpu.SMEM((TROWS, SLOTS + 8), jnp.int32),
             pltpu.SMEM((TROWS,), jnp.int32),
-            pltpu.SemaphoreType.DMA((6,)),
+            pltpu.SemaphoreType.DMA(()),
         ],
         compiler_params=PARAMS,
         name="backward",
-    )(trow, dslot, count, coef, cot_rows, stacked, tile_values)
+    )(trow, dslot, count, coef, *map(near, (cot_rows, stacked, tile_values)))
 
 
 def forward_kernel(
-    trow, xslot, count, half, coef, relc, relr, xmine, xother, tiles_in, grads_in, bases_in, cot_in,
+    trow, xslot, count, half, coef, relc, relr, xmine, xother, tiles_in, grads_in, bases_in, cot,
     outp, dkeep, dgive, coefg,
-    feats, tiles, grads, bases, cot, sums, part, msg, gram, order, filled, sems,
+    feats, tiles, grads, bases, sums, part, msg, gram, order, filled, sems,
 ):
     loads = [
         pltpu.make_async_copy(src, dst, sems.at[k])
         for k, (src, dst) in enumerate(
             (
-                (tiles_in, tiles),
                 (xmine, feats.at[pl.ds(0, SLOTS)]),
                 (xother, feats.at[pl.ds(SLOTS, SLOTS)]),
+                (tiles_in, tiles),
                 (grads_in, grads),
                 (bases_in, bases),
-                (cot_in, cot),
             )
         )
     ]
@@ -172,13 +160,15 @@
     msg[SLOTS] = jnp.zeros((TILE, H), F32)
     gram[...] = jnp.zeros_like(gram)
     by_row(trow, count, order, filled)
-    for copy in loads[:4]:
+    for copy in loads[:3]:
         copy.wait()
+
     def message(s):
         m = jnp.dot(tiles[s], feats[xslot[s]], preferred_element_type=F32).astype(BF16)
         msg[s] = m.astype(F32)
 
     fours(count, message)
+    loads[3].wait()
 
     def add(t, s1, s2):
         c1 = [coef[s1, b] for b in range(B)]
@@ -200,11 +190,10 @@
 
     pairs(order, filled, add)
 
-    for copy in loads[4:]:
-        copy.wait()
     for t in range(TROWS):
         for b in range(B):
             part[pl.ds(t * TILE, TILE), pl.ds(b * H, H)] = sums[t, b].astype(BF16)
+    loads[4].wait()
     outp[...] = jnp.dot(part[...], bases[...], preferred_element_type=F32).astype(BF16)
     mine = half[0]
 
@@ -236,31 +225,33 @@
 def forward(trow, xslot, count, half, coef, relc, relr, xmine, xother, tiles, grads, stacked, cot_rows):
     return pl.pallas_call(
         forward_kernel,
-        in_specs=[SMEM] * 5 + [VMEM] * 2 + [ANY] * 6,
+        in_specs=[SMEM] * 5 + [VMEM] * 2 + [ANY] * 5 + [VMEM],
         out_specs=[VMEM] * 4,
         out_shape=[
-            jax.ShapeDtypeStruct((TROWS * TILE, H), BF16),
-            jax.ShapeDtypeStruct((1024, H), F32),
-            jax.ShapeDtypeStruct((1056, H), BF16),
-            jax.ShapeDtypeStruct((32, 128), F32),
+            pltpu.VMEM((TROWS * TILE, H), BF16),
+            pltpu.VMEM((1024, H), F32),
+            pltpu.VMEM((1056, H), BF16),
+            pltpu.VMEM((32, 128), F32),
         ],
         scratch_shapes=[
             pltpu.VMEM((2 * SLOTS, TILE, H), BF16),
             pltpu.VMEM((SLOTS, TILE, TILE), BF16),
             pltpu.VMEM((TROWS, B, TILE, H), BF16),
             pltpu.VMEM((B * H, H), BF16),
-            pltpu.VMEM((TROWS * TILE, H), BF16),
             pltpu.VMEM((TROWS, B, TILE, H), F32),
             pltpu.VMEM((TROWS * TILE, B * H), BF16),
             pltpu.VMEM((SLOTS + 1, TILE, H), F32),
             pltpu.VMEM((SLOTS + 1, B, 8, 128), F32),
             pltpu.SMEM((TROWS, SLOTS + 8), jnp.int32),
             pltpu.SMEM((TROWS,), jnp.int32),
-            pltpu.SemaphoreType.DMA((6,)),
+            pltpu.SemaphoreType.DMA((5,)),
         ],
         compiler_params=PARAMS,
         name="forward",
-    )(trow, xslot, count, half, coef, relc, relr, xmine, xother, tiles, grads, stacked, cot_rows)
+    )(
+        trow, xslot, count, half, coef, relc, relr,
+        *map(far, (xmine, xother, tiles, grads, stacked)), near(cot_rows),
+    )
 
 
 def swap(x):
@@ -345,11 +336,12 @@
     dv = (dkeep + dgot[:1024].astype(F32)).reshape(NX, 256, H).astype(BF16)
     cg = coefg + dgot[1024:, :128].astype(F32) + dgot[1024:, 128:].astype(F32)
     cg_x = jnp.broadcast_to(two_parts(cg)[None], (NX, 32, H))
-    with jax.named_scope("dv_x"):
-        got_x = exchange(jnp.concatenate([dv, outp.reshape(NX, TILE, H), cg_x], axis=1), "x")
-    got_x, dx = after(got_x, dx)
+    send_x = jnp.concatenate([dv, outp.reshape(NX, TILE, H), cg_x], axis=1)
+    send_x, dx = after(send_x, dx)
     with jax.named_scope("dx_z"):
         dx = lax.psum_scatter(dx.astype(F32), "z", scatter_dimension=0, tiled=True)
+    with jax.named_scope("dv_x"):
+        got_x = exchange(send_x, "x")
     sum_x = jnp.sum(got_x.astype(F32), axis=0)
     layer_out = sum_x[256:384].astype(BF16)
     cg = sum_x[384:, :128] + sum_x[384:, 128:]
@@ -369,9 +361,9 @@
     scale = (NY * NZ * NC * NX * TILE) ** (-0.5)
     cg = all_yz[:, 8, :128].astype(F32) + all_yz[:, 8, 128:].astype(F32)
     grad_coef = (cg * scale).reshape(512, B)[:RELS]
+    all_yz, dx = after(all_yz, dx)
     with jax.named_scope("all_x"):
         all_x = spread_to(all_yz[:, :8].reshape(256, H), "x", NX).reshape(1024, H)
-    all_x, dx = after(all_x, dx)
     with jax.named_scope("all_c"):
         all_other = swap(all_x)
     first = jnp.where(mine == 0, all_x, all_other)

time: 173 us -> 163 us (0.942)
  blocking collectives: 48.9 us -> 65.7 us
  waiting for transfers between devices: 39.6 us -> 32.8 us
  starting transfers between devices: 25.1 us -> 18.7 us
  Pallas kernels: 19.3 us -> 14 us
  other arithmetic: 13.1 us -> 8.97 us
  local copies, waits for them, and re-layouts: 5.21 us -> 2.68 us
    all_to_all x3 -> x4, blocking collectives: 36.5 us -> 55.8 us  [exchange(): return lax.all_to_all(x, axes, split_axis=0, concat_axis=0, tiled=True)]
    all_to_all x2 -> x1, waiting for transfers between devices: 20.9 us -> 9.84 us  [exchange(): return lax.all_to_all(x, axes, split_axis=0, concat_axis=0, tiled=True)]
    all_to_all x2 -> x1, starting transfers between devices: 13.6 us -> 3.97 us  [exchange(): return lax.all_to_all(x, axes, split_axis=0, concat_axis=0, tiled=True)]
    all_gather x1, waiting for transfers between devices: 4.69 us -> 11.5 us  [local(): feats_mine = lax.all_gather(feats_y, 'z', axis=0, tiled=True)]
    reduce_scatter x1, waiting for transfers between devices: 5.91 us -> 0.01 us  [local(): dx = lax.psum_scatter(dx.astype(F32), 'z', scatter_dimension=0, tiled=True)]
    ppermute x4, starting transfers between devices: 11.3 us -> 14.7 us  [swap(): return lax.ppermute(x, 'c', [(0, 1), (1, 0)])]
    pallas_call x1, Pallas kernels: 7.92 us -> 5.21 us  [backward(): pl.pallas_call(backward_kernel, in_specs=[SMEM] * 4 + [VMEM] * 3, out_spe...]
    pallas_call x1, Pallas kernels: 11.4 us -> 8.8 us  [forward(): pl.pallas_call(forward_kernel, in_specs=[SMEM] * 5 + [VMEM] * 2 + [ANY] *...]
  transfers between devices with their start and end apart: 9 -> 8, of which waited for: 7 -> 6; matrix products, arithmetic and copies ran while one was open for 10% -> 7% of each run, Pallas kernels for 11% -> 9%
where the time goes in v4:
time: 163 us; the launch traced here: 162 us
  blocking collectives  65.7 us (40%)
  waiting for transfers between devices  32.8 us (20%)
  starting transfers between devices  18.7 us (11%)
  between operations  16.4 us (10%)
  Pallas kernels  14 us (9%)
  other arithmetic  8.97 us (6%)
  matrix products  2.91 us (2%)
  local copies, waits for them, and re-layouts  2.68 us (2%)
    all_to_all x4, blocking collectives, exchange(): return lax.all_to_all(x, axes, split_axis=0, concat_axis=0, tiled=True)  55.8 us
    ppermute x4, starting transfers between devices, swap(): return lax.ppermute(x, 'c', [(0, 1), (1, 0)])  14.7 us
    all_gather x1, waiting for transfers between devices, local(): feats_mine = lax.all_gather(feats_y, 'z', axis=0, tiled=True)  11.5 us
    all_gather x1, blocking collectives, local(): cot_rows = lax.all_gather(cotangent, 'x', axis=0, tiled=True)  9.96 us
    all_to_all x1, waiting for transfers between devices, exchange(): return lax.all_to_all(x, axes, split_axis=0, concat_axis=0, tiled=True)  9.84 us
    ppermute x4, waiting for transfers between devices, swap(): return lax.ppermute(x, 'c', [(0, 1), (1, 0)])  9.56 us
    pallas_call x1, Pallas kernels, forward(): pl.pallas_call(forward_kernel, in_specs=[SMEM] * 5 + [VMEM] * 2 + [ANY] *...  8.8 us
    pallas_call x1, Pallas kernels, backward(): pl.pallas_call(backward_kernel, in_specs=[SMEM] * 4 + [VMEM] * 3, out_spe...  5.21 us
  transfers between devices with their start and end apart: 8, of which 6 were waited for; matrix products, arithmetic and copies ran while one was open for 7% of the time, Pallas kernels for 9%

profile of v4, /device:TPU:1, one launch (start us, length us, event | category | flops | bytes accessed | tf_op | source)
XLA Modules:
  0.0 162.2 jit_solution(4510222154060923393)
XLA Ops:
  8.1 0.9 convert_reduce_fusion.2
  9.0 1.0 fusion
  10.0 10.4 %all_to_all.25 = bf16[4,128,256]{2,1,0:T(8,128)(2,1)} all-to-all(bf16[4,128,256]{2,1,0:T(8,128)(2,1)S(1)} %broadcast_in_dim.20), channel_id=1, replica_groups=mesh['y'=4,'z'=8,'c'=2,'x'=4] {'y'}, dimensions={0} | all-to-all | bytes 524288 | tf_op jit(solution)/shard_map/feats_y/all_to_all | solution.py:262
  21.2 0.7 pad.4
  21.9 0.7 add_add_fusion
  22.5 0.9 fusion.3.coef
  23.4 10.0 %all_gather.7.cot = bf16[512,256]{1,0:T(8,128)(2,1)S(1)} all-gather(bf16[128,256]{1,0:T(8,128)(2,1)} %param.19), channel_id=1, replica_groups=mesh['y'=4,'z'=8,'c'=2,'x'=4] {'x'}, dimensions={0}, use_global_device_ids=true | all-gather | bytes 327680 | tf_op jit(solution)/shard_map/cot_x/all_gather | solution.py:314
  33.4 5.2 %backward.1 = (bf16[4,8,128,256]{3,2,1,0:T(8,128)(2,1)}, bf16[32,128,256]{2,1,0:T(8,128)(2,1)S(1)}, bf16[32,128,256]{2,1,0:T(8,128)(2,1)S(1)}) custom-call(s32[32]{0:T(128)S(1)} %copy-done.3, s32[32]{0:T(128)S(1)} %get-tuple-element.42.dslot, s32[1]{0:T(128)S(6)} %copy.33.count, f32[40,8]{1,0:T(8,128)S(1)} %fusion.3.coef, ...), custom_call_target="tpu_custom_call" | custom-call | tf_op jit(solution)/shard_map/backward/pallas_call | solution.py:121
  38.6 4.4 %collective-permute-start.2 = (bf16[32,128,256]{2,1,0:T(8,128)(2,1)S(1)}, bf16[32,128,256]{2,1,0:T(8,128)(2,1)S(1)}, u32[]{:S(2)}, u32[]{:S(2)}) collective-permute-start(bf16[32,128,256]{2,1,0:T(8,128)(2,1)S(1)} %get-tuple-element.25), channel_id=1, source_target_pairs={{0,4},{4,0},{1,5},{5,1},{2,6},{6,2},{3,7},{7,3},{8,12},{12,8},{9,1... | collective-permute-start | bytes 6291464 | tf_op jit(solution)/shard_map/dx_c/ppermute | solution.py:258
  43.1 3.8 %collective-permute-done.2 = bf16[32,128,256]{2,1,0:T(8,128)(2,1)S(1)} collective-permute-done((bf16[32,128,256]{2,1,0:T(8,128)(2,1)S(1)}, bf16[32,128,256]{2,1,0:T(8,128)(2,1)S(1)}, u32[]{:S(2)}, u32[]{:S(2)}) %collective-permute-start.2) | collective-permute-done | bytes 2097184 | tf_op jit(solution)/shard_map/dx_c/ppermute | solution.py:258
  46.8 2.1 %add_convert_fusion = bf16[32,128,256]{2,1,0:T(8,128)(2,1)} fusion(bf16[32,128,256]{2,1,0:T(8,128)(2,1)S(1)} %collective-permute-done.2, bf16[32,128,256]{2,1,0:T(8,128)(2,1)S(1)} %get-tuple-element.24), kind=kLoop, calls=%fused_computation | loop fusion | flops 4194304 | bytes 6291456 | tf_op jit(solution)/shard_map/convert_element_type | solution.py:321
  49.0 11.5 %all-gather.2.cloned.1.call-done = bf16[4096,256]{1,0:T(8,128)(2,1)} async-done(((bf16[512,256]{1,0:T(8,128)(2,1)}), bf16[4096,256]{1,0:T(8,128)(2,1)}) %all-gather.2.cloned.1.call-update) | async-done | bytes 2097168 | tf_op jit(solution)/shard_map/feats_z/all_gather | solution.py:312
  60.4 4.6 %collective-permute-start = (bf16[32,128,256]{2,1,0:T(8,128)(2,1)}, bf16[32,128,256]{2,1,0:T(8,128)(2,1)}, u32[]{:S(2)}, u32[]{:S(2)}) collective-permute-start(bf16[32,128,256]{2,1,0:T(8,128)(2,1)} %bitcast.29), channel_id=1, source_target_pairs={{0,4},{4,0},{1,5},{5,1},{2,6},{6,2},{3,7},{7,3},{8,12},{12,8},{9,1... | collective-permute-start | bytes 6291464 | tf_op jit(solution)/shard_map/feats_c/ppermute | solution.py:258
  65.3 3.9 %collective-permute-done.xother = bf16[32,128,256]{2,1,0:T(8,128)(2,1)} collective-permute-done((bf16[32,128,256]{2,1,0:T(8,128)(2,1)}, bf16[32,128,256]{2,1,0:T(8,128)(2,1)}, u32[]{:S(2)}, u32[]{:S(2)}) %collective-permute-start) | collective-permute-done | bytes 2097184 | tf_op jit(solution)/shard_map/feats_c/ppermute | solution.py:258
  69.2 8.8 %forward.1 = (bf16[512,256]{1,0:T(8,128)(2,1)S(1)}, f32[1024,256]{1,0:T(8,128)S(1)}, bf16[1056,256]{1,0:T(8,128)(2,1)S(1)}, f32[32,128]{1,0:T(8,128)S(1)}) custom-call(s32[32]{0:T(128)S(1)} %copy-done.3, s32[32]{0:T(128)S(1)} %add_add_fusion.1.xslot, s32[1]{0:T(128)S(6)} %copy.33.count, s32[1]{0:T(128)} %bitcast.half, f32[40,8]{1,0:T(8,128)S(1)} %fusion.3.coef, ...), custom_call_target="tpu_custom_call" | custom-call | tf_op jit(solution)/shard_map/forward/pallas_call | solution.py:226
  78.1 1.9 %collective-permute-done.1 = bf16[1056,256]{1,0:T(8,128)(2,1)S(1)} collective-permute-done((bf16[1056,256]{1,0:T(8,128)(2,1)S(1)}, bf16[1056,256]{1,0:T(8,128)(2,1)S(1)}, u32[]{:S(2)}, u32[]{:S(2)}) %collective-permute-start.1) | collective-permute-done | bytes 540704 | tf_op jit(solution)/shard_map/dv_c/ppermute | solution.py:258
  80.0 0.1 add_convert_fusion.1
  80.2 1.0 pad_maximum_fusion
  81.2 1.9 %reduce-scatter.3.cloned.1.call-done = bf16[1024,256]{1,0:T(8,128)(2,1)} async-done(((bf16[4096,256]{1,0:T(8,128)(2,1)}), bf16[1024,256]{1,0:T(8,128)(2,1)}) %reduce-scatter.3.cloned.1.call-update) | async-done | bytes 524304 | tf_op jit(solution)/shard_map/dx_y/reduce_scatter | solution.py:323
  83.1 4.0 %all-to-all-start.1 = ((bf16[4,416,256]{2,1,0:T(8,128)(2,1)}), bf16[4,416,256]{2,1,0:T(8,128)(2,1)S(1)}, u32[]{:S(2)}, u32[]{:S(2)}) async-start(bf16[4,416,256]{2,1,0:T(8,128)(2,1)} %pad_maximum_fusion), calls=%async_computation.2 | async-start | bytes 1703936 | tf_op jit(solution)/shard_map/dv_x/all_to_all | solution.py:262
  87.1 2.1 %convert_element_type.99 = f32[1024,256]{1,0:T(8,128)} convert(bf16[1024,256]{1,0:T(8,128)(2,1)} %reduce-scatter.3.cloned.1.call-done) | non-fusion elementwise | flops 262144 | bytes 1572864 | tf_op jit(solution)/shard_map/dx_z/convert_element_type | solution.py:342
  89.2 9.8 %all-to-all-done.1 = bf16[4,416,256]{2,1,0:T(8,128)(2,1)S(1)} async-done(((bf16[4,416,256]{2,1,0:T(8,128)(2,1)}), bf16[4,416,256]{2,1,0:T(8,128)(2,1)S(1)}, u32[]{:S(2)}, u32[]{:S(2)}) %all-to-all-start.1) | async-done | bytes 852000 | tf_op jit(solution)/shard_map/dv_x/all_to_all | solution.py:262
  99.1 0.1 convert_reduce_fusion
  99.4 19.7 %all_to_all.26 = bf16[32,16,256]{2,1,0:T(8,128)(2,1)S(1)} all-to-all(bf16[32,16,256]{2,1,0:T(8,128)(2,1)S(1)} %maximum_maximum_fusion), channel_id=1, replica_groups=mesh['y'=4,'z'=8,'c'=2,'x'=4] {'y','z'}, dimensions={0} | all-to-all | bytes 524288 | tf_op jit(solution)/shard_map/dv_yz/all_to_all | solution.py:262
  119.2 16.3 %all_to_all.27 = bf16[32,16,256]{2,1,0:T(8,128)(2,1)S(1)} all-to-all(bf16[32,16,256]{2,1,0:T(8,128)(2,1)S(1)} %broadcast_in_dim.24), channel_id=1, replica_groups=mesh['y'=4,'z'=8,'c'=2,'x'=4] {'y','z'}, dimensions={0} | all-to-all | bytes 524288 | tf_op jit(solution)/shard_map/all_yz/all_to_all | solution.py:262
  135.6 9.4 %all_to_all.28 = bf16[4,256,256]{2,1,0:T(8,128)(2,1)S(1)} all-to-all(bf16[4,256,256]{2,1,0:T(8,128)(2,1)S(1)} %broadcast_in_dim.52), channel_id=1, replica_groups=mesh['y'=4,'z'=8,'c'=2,'x'=4] {'x'}, dimensions={0} | all-to-all | bytes 1048576 | tf_op jit(solution)/shard_map/all_x/all_to_all | solution.py:262
  145.0 5.5 %collective-permute-start.3 = (bf16[1024,256]{1,0:T(8,128)(2,1)S(1)}, bf16[1024,256]{1,0:T(8,128)(2,1)S(1)}, u32[]{:S(2)}, u32[]{:S(2)}) collective-permute-start(bf16[1024,256]{1,0:T(8,128)(2,1)S(1)} %bitcast.31), channel_id=1, source_target_pairs={{0,4},{4,0},{1,5},{5,1},{2,6},{6,2},{3,7},{7,3},{8,12},{12,8},{9,1... | collective-permute-start | bytes 1572872 | tf_op jit(solution)/shard_map/all_c/ppermute | solution.py:258
  150.5 0.6 slice.62
  151.2 0.2 mul.46
  151.4 0.7 copy.31
  152.1 1.0 fusion.1
  153.3 1.5 convert_multiply_fusion
  (49 shorter events, 1.2 us)
Async XLA Ops:
  8.0 1.0 copy-start
  8.0 25.4 %copy-start.2 = (bf16[8,256,256]{2,1,0:T(8,128)(2,1)S(1)}, bf16[8,256,256]{2,1,0:T(8,128)(2,1)}, u32[]{:S(2)}) copy-start(bf16[8,256,256]{2,1,0:T(8,128)(2,1)} %param.18) | copy-start | bytes 3145732
  8.0 25.4 %copy-start.1 = (bf16[32,128,128]{2,1,0:T(8,128)(2,1)S(1)}, bf16[32,128,128]{2,1,0:T(8,128)(2,1)}, u32[]{:S(2)}) copy-start(bf16[32,128,128]{2,1,0:T(8,128)(2,1)} %tiles_in.1) | copy-start | bytes 3145732
  8.0 25.4 %copy-start.3 = (s32[32]{0:T(128)S(1)}, s32[32]{0:T(128)}, u32[]{:S(2)}) copy-start(s32[32]{0:T(128)} %trow.3) | copy-start | bytes 388
  8.0 52.4 %all-gather.2.cloned.1.call-start = ((), (), s32[]{:S(2)}) async-start(), calls=%async_computation.7 | async-start | bytes 2359296 | tf_op jit(solution)/shard_map/feats_z/all_gather | solution.py:312
  20.5 62.6 %reduce-scatter.3.cloned.1.call-start = ((), (), s32[]{:S(2)}) async-start(), calls=%async_computation.8 | async-start | bytes 2621440 | tf_op jit(solution)/shard_map/dx_y/reduce_scatter | solution.py:323
  38.6 8.2 %collective-permute-start.2 = (bf16[32,128,256]{2,1,0:T(8,128)(2,1)S(1)}, bf16[32,128,256]{2,1,0:T(8,128)(2,1)S(1)}, u32[]{:S(2)}, u32[]{:S(2)}) collective-permute-start(bf16[32,128,256]{2,1,0:T(8,128)(2,1)S(1)} %get-tuple-element.25), channel_id=1, source_target_pairs={{0,4},{4,0},{1,5},{5,1},{2,6},{6,2},{3,7},{7,3},{8,12},{12,8},{9,1... | collective-permute-start | bytes 6291464 | tf_op jit(solution)/shard_map/dx_c/ppermute | solution.py:258
  48.9 16.1 %copy-start.4 = (s32[32]{0:T(128)S(1)}, s32[32]{0:T(128)}, u32[]{:S(2)}) copy-start(s32[32]{0:T(128)} %param.15) | copy-start | bytes 388
  60.4 8.7 %collective-permute-start = (bf16[32,128,256]{2,1,0:T(8,128)(2,1)}, bf16[32,128,256]{2,1,0:T(8,128)(2,1)}, u32[]{:S(2)}, u32[]{:S(2)}) collective-permute-start(bf16[32,128,256]{2,1,0:T(8,128)(2,1)} %bitcast.29), channel_id=1, source_target_pairs={{0,4},{4,0},{1,5},{5,1},{2,6},{6,2},{3,7},{7,3},{8,12},{12,8},{9,1... | collective-permute-start | bytes 6291464 | tf_op jit(solution)/shard_map/feats_c/ppermute | solution.py:258
  78.0 2.0 %collective-permute-start.1 = (bf16[1056,256]{1,0:T(8,128)(2,1)S(1)}, bf16[1056,256]{1,0:T(8,128)(2,1)S(1)}, u32[]{:S(2)}, u32[]{:S(2)}) collective-permute-start(bf16[1056,256]{1,0:T(8,128)(2,1)S(1)} %get-tuple-element.21), channel_id=1, source_target_pairs={{0,4},{4,0},{1,5},{5,1},{2,6},{6,2},{3,7},{7,3},{8,12},{12,8},{9,1... | collective-permute-start | bytes 1622024 | tf_op jit(solution)/shard_map/dv_c/ppermute | solution.py:258
  83.1 16.0 %all-to-all-start.1 = ((bf16[4,416,256]{2,1,0:T(8,128)(2,1)}), bf16[4,416,256]{2,1,0:T(8,128)(2,1)S(1)}, u32[]{:S(2)}, u32[]{:S(2)}) async-start(bf16[4,416,256]{2,1,0:T(8,128)(2,1)} %pad_maximum_fusion), calls=%async_computation.2 | async-start | bytes 1703936 | tf_op jit(solution)/shard_map/dv_x/all_to_all | solution.py:262
  87.0 48.5 %reduce-scatter.5.cloned.1.call-start = ((), (), s32[]{:S(2)}) async-start(), calls=%async_computation.9 | async-start | bytes 1179648 | tf_op jit(solution)/shard_map/dx_z/reduce_scatter | solution.py:342
  119.1 33.0 %copy-start.6 = (s32[256]{0:T(256)S(1)}, s32[256]{0:T(256)}, u32[]{:S(2)}) copy-start(s32[256]{0:T(256)} %param.11) | copy-start | bytes 3076
  135.5 16.6 %copy-start.5 = (f32[128,256]{1,0:T(8,128)S(1)}, f32[128,256]{1,0:T(8,128)}, u32[]{:S(2)}) copy-start(f32[128,256]{1,0:T(8,128)} %reduce-scatter.5.cloned.1.call-done) | copy-start | bytes 393220
  145.0 8.2 %collective-permute-start.3 = (bf16[1024,256]{1,0:T(8,128)(2,1)S(1)}, bf16[1024,256]{1,0:T(8,128)(2,1)S(1)}, u32[]{:S(2)}, u32[]{:S(2)}) collective-permute-start(bf16[1024,256]{1,0:T(8,128)(2,1)S(1)} %bitcast.31), channel_id=1, source_target_pairs={{0,4},{4,0},{1,5},{5,1},{2,6},{6,2},{3,7},{7,3},{8,12},{12,8},{9,1... | collective-permute-start | bytes 1572872 | tf_op jit(solution)/shard_map/all_c/ppermute | solution.py:258
Sparse Core Ops, SparseCore 0:
  20.6 39.7 all-gather.1
  91.1 37.8 reduce-scatter.4
Sparse Core Ops, SparseCore 1:
  49.0 34.0 reduce-scatter.2

commit v5 on v4

--- a/solution.py
+++ b/solution.py
@@ -19,7 +19,7 @@
 VMEM = pl.BlockSpec(memory_space=pltpu.VMEM)
 SMEM = pl.BlockSpec(memory_space=pltpu.SMEM)
 ANY = pl.BlockSpec(memory_space=pl.ANY)
-PARAMS = pltpu.CompilerParams(vmem_limit_bytes=32 * 2**20)
+PARAMS = pltpu.CompilerParams(vmem_limit_bytes=24 * 2**20)
 
 
 def far(x):
@@ -138,9 +138,9 @@
 
 
 def forward_kernel(
-    trow, xslot, count, half, coef, relc, relr, xmine, xother, tiles_in, grads_in, bases_in, cot,
-    outp, dkeep, dgive, coefg,
-    feats, tiles, grads, bases, sums, part, msg, gram, order, filled, sems,
+    trow, xslot, count, half, coef, xmine, xother, tiles, bases, cot,
+    outp, dkeep, dgive, sent,
+    feats, sums, part, msg, short, order, filled, sems,
 ):
     loads = [
         pltpu.make_async_copy(src, dst, sems.at[k])
@@ -148,9 +148,6 @@
             (
                 (xmine, feats.at[pl.ds(0, SLOTS)]),
                 (xother, feats.at[pl.ds(SLOTS, SLOTS)]),
-                (tiles_in, tiles),
-                (grads_in, grads),
-                (bases_in, bases),
             )
         )
     ]
@@ -158,29 +155,103 @@
         copy.start()
     sums[...] = jnp.zeros_like(sums)
     msg[SLOTS] = jnp.zeros((TILE, H), F32)
-    gram[...] = jnp.zeros_like(gram)
+    short[...] = jnp.zeros_like(short)
     by_row(trow, count, order, filled)
-    for copy in loads[:3]:
+    for copy in loads:
         copy.wait()
 
     def message(s):
         m = jnp.dot(tiles[s], feats[xslot[s]], preferred_element_type=F32).astype(BF16)
+        short[s] = m
         msg[s] = m.astype(F32)
 
     fours(count, message)
-    loads[3].wait()
+    store = pltpu.make_async_copy(short, sent, sems.at[2])
+    store.start()
 
     def add(t, s1, s2):
         c1 = [coef[s1, b] for b in range(B)]
         c2 = [coef[s2, b] for b in range(B)]
-        d1 = [jnp.zeros((8, 128), F32)] * B
-        d2 = [jnp.zeros((8, 128), F32)] * B
         for r in range(8):
             rows = pl.ds(r * 16, 16)
             m1 = msg[s1, rows, :]
             m2 = msg[s2, rows, :]
             for b in range(B):
                 sums[t, b, rows, :] = sums[t, b, rows, :] + (c1[b] * m1 + c2[b] * m2)
+
+    pairs(order, filled, add)
+
+    for t in range(TROWS):
+        for b in range(B):
+            part[pl.ds(t * TILE, TILE), pl.ds(b * H, H)] = sums[t, b].astype(BF16)
+    outp[...] = jnp.dot(part[...], bases[...], preferred_element_type=F32).astype(BF16)
+    mine = half[0]
+
+    def outer(k):
+        cols = pl.ds(pl.multiple_of(k * H, H), H)
+        return lax.dot_general(
+            part[:, cols], cot[...], (((0,), (0,)), ((), ())), preferred_element_type=F32
+        )
+
+    for k in range(B // 2):
+        rows = pl.ds(k * H, H)
+        dkeep[rows, :] = outer(mine * (B // 2) + k)
+        dgive[rows, :] = outer((1 - mine) * (B // 2) + k).astype(BF16)
+    store.wait()
+
+
+def forward(trow, xslot, count, half, coef, xmine, xother, tiles, stacked, cot_rows):
+    return pl.pallas_call(
+        forward_kernel,
+        in_specs=[SMEM] * 5 + [ANY] * 2 + [VMEM] * 3,
+        out_specs=[VMEM] * 3 + [ANY],
+        out_shape=[
+            pltpu.VMEM((TROWS * TILE, H), BF16),
+            pltpu.VMEM((1024, H), F32),
+            pltpu.VMEM((1024, H), BF16),
+            pltpu.HBM((SLOTS, TILE, H), BF16),
+        ],
+        scratch_shapes=[
+            pltpu.VMEM((2 * SLOTS, TILE, H), BF16),
+            pltpu.VMEM((TROWS, B, TILE, H), F32),
+            pltpu.VMEM((TROWS * TILE, B * H), BF16),
+            pltpu.VMEM((SLOTS + 1, TILE, H), F32),
+            pltpu.VMEM((SLOTS, TILE, H), BF16),
+            pltpu.SMEM((TROWS, SLOTS + 8), jnp.int32),
+            pltpu.SMEM((TROWS,), jnp.int32),
+            pltpu.SemaphoreType.DMA((3,)),
+        ],
+        compiler_params=PARAMS,
+        name="forward",
+    )(
+        trow, xslot, count, half, coef,
+        *map(far, (xmine, xother)), *map(near, (tiles, stacked, cot_rows)),
+    )
+
+
+def gram_kernel(
+    trow, count, relc, relr, sent, grads_in, coefg, msg, grads, gram, order, filled, sems
+):
+    loads = [
+        pltpu.make_async_copy(sent, msg.at[pl.ds(0, SLOTS)], sems.at[0]),
+        pltpu.make_async_copy(grads_in, grads, sems.at[1]),
+    ]
+    for copy in loads:
+        copy.start()
+    msg[SLOTS] = jnp.zeros((TILE, H), BF16)
+    gram[...] = jnp.zeros_like(gram)
+    by_row(trow, count, order, filled)
+    for copy in loads:
+        copy.wait()
+
+    def dots(t, s1, s2):
+        d1 = [jnp.zeros((8, 128), F32)] * B
+        d2 = [jnp.zeros((8, 128), F32)] * B
+        for r in range(8):
+            rows = pl.ds(r * 16, 16)
+            m1 = msg[s1, rows, :].astype(F32)
+            m2 = msg[s2, rows, :].astype(F32)
+            for b in range(B):
                 g = grads[t, b, rows, :].astype(F32)
                 d1[b] = d1[b] + fold(m1 * g)
                 d2[b] = d2[b] + fold(m2 * g)
@@ -188,26 +259,7 @@
             gram[s1, b] = d1[b]
             gram[s2, b] = d2[b]
 
-    pairs(order, filled, add)
-
-    for t in range(TROWS):
-        for b in range(B):
-            part[pl.ds(t * TILE, TILE), pl.ds(b * H, H)] = sums[t, b].astype(BF16)
-    loads[4].wait()
-    outp[...] = jnp.dot(part[...], bases[...], preferred_element_type=F32).astype(BF16)
-    mine = half[0]
-
-    def outer(k):
-        cols = pl.ds(pl.multiple_of(k * H, H), H)
-        return lax.dot_general(
-            part[:, cols], cot[...], (((0,), (0,)), ((), ())), preferred_element_type=F32
-        )
-
-    for k in range(B // 2):
-        rows = pl.ds(k * H, H)
-        dkeep[rows, :] = outer(mine * (B // 2) + k)
-        dgive[rows, :] = outer((1 - mine) * (B // 2) + k).astype(BF16)
-
+    pairs(order, filled, dots)
     col = jnp.sum(jnp.sum(gram[pl.ds(0, SLOTS)].reshape(SLOTS * B, 8, 128), axis=1), axis=1, keepdims=True)
     lane = lax.broadcasted_iota(jnp.int32, (SLOTS * B, 128), 1)
     row = lax.broadcasted_iota(jnp.int32, (SLOTS * B, 128), 0)
@@ -217,41 +269,25 @@
     gather = (relr[...] // 16 == line).astype(F32)
     cg = jnp.dot(gather, spread, precision=lax.Precision.HIGHEST, preferred_element_type=F32)
     coefg[...] = cg
-    hi = cg.astype(BF16)
-    dgive[pl.ds(1024, 32), pl.ds(0, 128)] = hi
-    dgive[pl.ds(1024, 32), pl.ds(128, 128)] = (cg - hi.astype(F32)).astype(BF16)
-
-
-def forward(trow, xslot, count, half, coef, relc, relr, xmine, xother, tiles, grads, stacked, cot_rows):
+
+
+def gram_sums(trow, count, relc, relr, sent, grads):
     return pl.pallas_call(
-        forward_kernel,
-        in_specs=[SMEM] * 5 + [VMEM] * 2 + [ANY] * 5 + [VMEM],
-        out_specs=[VMEM] * 4,
-        out_shape=[
-            pltpu.VMEM((TROWS * TILE, H), BF16),
-            pltpu.VMEM((1024, H), F32),
-            pltpu.VMEM((1056, H), BF16),
-            pltpu.VMEM((32, 128), F32),
-        ],
+        gram_kernel,
+        in_specs=[SMEM] * 2 + [VMEM] * 2 + [ANY] * 2,
+        out_specs=VMEM,
+        out_shape=jax.ShapeDtypeStruct((32, 128), F32),
         scratch_shapes=[
-            pltpu.VMEM((2 * SLOTS, TILE, H), BF16),
-            pltpu.VMEM((SLOTS, TILE, TILE), BF16),
+            pltpu.VMEM((SLOTS + 1, TILE, H), BF16),
             pltpu.VMEM((TROWS, B, TILE, H), BF16),
-            pltpu.VMEM((B * H, H), BF16),
-            pltpu.VMEM((TROWS, B, TILE, H), F32),
-            pltpu.VMEM((TROWS * TILE, B * H), BF16),
-            pltpu.VMEM((SLOTS + 1, TILE, H), F32),
             pltpu.VMEM((SLOTS + 1, B, 8, 128), F32),
             pltpu.SMEM((TROWS, SLOTS + 8), jnp.int32),
             pltpu.SMEM((TROWS,), jnp.int32),
-            pltpu.SemaphoreType.DMA((5,)),
+            pltpu.SemaphoreType.DMA((2,)),
         ],
         compiler_params=PARAMS,
-        name="forward",
-    )(
-        trow, xslot, count, half, coef, relc, relr,
-        *map(far, (xmine, xother, tiles, grads, stacked)), near(cot_rows),
-    )
+        name="gram",
+    )(trow, count, relc, relr, far(sent), far(grads))
 
 
 def swap(x):
@@ -269,6 +305,10 @@
 def two_parts(x):
     hi = lax.reduce_precision(x, 8, 7)
     return jnp.concatenate([hi, x - hi], axis=-1).astype(BF16)
+
+
+def one_part(x):
+    return x[..., :128] + x[..., 128:]
 
 
 def after(x, y):
@@ -326,25 +366,24 @@
     with jax.named_scope("feats_c"):
         feats_other = swap(feats_mine)
     rels = jnp.repeat(tile_rels, B)
-    outp, dkeep, dgive, coefg = forward(
-        tile_rows, xslot, tile_counts, mine[None], coef, rels[:, None], rels[None, :],
-        feats_mine, feats_other, tile_values, grads, stacked, cot_rows,
+    outp, dkeep, dgive, sent = forward(
+        tile_rows, xslot, tile_counts, mine[None], coef,
+        feats_mine, feats_other, tile_values, stacked, cot_rows,
     )
 
     with jax.named_scope("dv_c"):
         dgot = swap(dgive)
-    dv = (dkeep + dgot[:1024].astype(F32)).reshape(NX, 256, H).astype(BF16)
-    cg = coefg + dgot[1024:, :128].astype(F32) + dgot[1024:, 128:].astype(F32)
-    cg_x = jnp.broadcast_to(two_parts(cg)[None], (NX, 32, H))
-    send_x = jnp.concatenate([dv, outp.reshape(NX, TILE, H), cg_x], axis=1)
+    dv = (dkeep + dgot.astype(F32)).reshape(NX, 256, H).astype(BF16)
+    send_x = jnp.concatenate([dv, outp.reshape(NX, TILE, H)], axis=1)
     send_x, dx = after(send_x, dx)
+    sent, dx = after(sent, dx.astype(F32))
     with jax.named_scope("dx_z"):
-        dx = lax.psum_scatter(dx.astype(F32), "z", scatter_dimension=0, tiled=True)
+        dx = lax.psum_scatter(dx, "z", scatter_dimension=0, tiled=True)
     with jax.named_scope("dv_x"):
         got_x = exchange(send_x, "x")
-    sum_x = jnp.sum(got_x.astype(F32), axis=0)
-    layer_out = sum_x[256:384].astype(BF16)
-    cg = sum_x[384:, :128] + sum_x[384:, 128:]
+    cg = gram_sums(tile_rows, tile_counts, rels[:, None], rels[None, :], sent, grads)
+    (sum_x,) = lax.optimization_barrier((jnp.sum(got_x.astype(F32), axis=0),))
+    layer_out = sum_x[256:].astype(BF16)
     pad = jnp.zeros((NY * NZ, 7, H), BF16)
     packed = jnp.concatenate(
         [sum_x[:256].reshape(NY * NZ, 8, H).astype(BF16), two_parts(cg)[:, None, :], pad], axis=1
@@ -352,22 +391,24 @@
     with jax.named_scope("dv_yz"):
         got_yz = exchange(packed, ("y", "z"))
     sum_yz = jnp.sum(got_yz.astype(F32), axis=0)
-    cg = sum_yz[8:9, :128] + sum_yz[8:9, 128:]
     packed = jnp.concatenate(
-        [sum_yz[:8].astype(BF16), two_parts(cg), jnp.zeros((7, H), BF16)], axis=0
+        [sum_yz[:8].astype(BF16), two_parts(one_part(sum_yz[8:9])), jnp.zeros((7, H), BF16)], axis=0
     )
     with jax.named_scope("all_yz"):
         all_yz = spread_to(packed, ("y", "z"), NY * NZ)
+    all_yz, dx = after(all_yz, dx)
+    send_x = jnp.concatenate([all_yz[:, :8].reshape(256, H), all_yz[:, 8]], axis=0)
+    with jax.named_scope("all_x"):
+        all_x = spread_to(send_x, "x", NX)
+    cg = two_parts(jnp.sum(one_part(all_x[:, 256:].astype(F32)), axis=0))
+    send_c = jnp.concatenate([all_x[:, :256].reshape(1024, H), cg], axis=0)
+    with jax.named_scope("all_c"):
+        got_c = swap(send_c)
     scale = (NY * NZ * NC * NX * TILE) ** (-0.5)
-    cg = all_yz[:, 8, :128].astype(F32) + all_yz[:, 8, 128:].astype(F32)
+    cg = one_part(send_c[1024:].astype(F32)) + one_part(got_c[1024:].astype(F32))
     grad_coef = (cg * scale).reshape(512, B)[:RELS]
-    all_yz, dx = after(all_yz, dx)
-    with jax.named_scope("all_x"):
-        all_x = spread_to(all_yz[:, :8].reshape(256, H), "x", NX).reshape(1024, H)
-    with jax.named_scope("all_c"):
-        all_other = swap(all_x)
-    first = jnp.where(mine == 0, all_x, all_other)
-    second = jnp.where(mine == 0, all_other, all_x)
+    first = jnp.where(mine == 0, send_c[:1024], got_c[:1024])
+    second = jnp.where(mine == 0, got_c[:1024], send_c[:1024])
     grad_bases = (jnp.stack([first, second]).astype(F32) * scale).reshape(B, H, H)
 
     quotient = dx / counts[:, None]

time: 163 us -> 164 us (level)
  waiting for transfers between devices: 32.8 us -> 29.5 us
  Pallas kernels: 14 us -> 16.5 us
    all_to_all x1, waiting for transfers between devices: 9.84 us -> 5.01 us  [exchange(): return lax.all_to_all(x, axes, split_axis=0, concat_axis=0, tiled=True)]
    pallas_call x1 -> x2, Pallas kernels: 8.8 us -> 11.6 us  [the longest x1 6.73 us: forward(): pl.pallas_call(forward_kernel, in_specs=[SMEM] * 5 + [ANY] * 2 + [VMEM] *...]
  transfers between devices with their start and end apart: 8 -> 8, of which waited for: 6 -> 6; matrix products, arithmetic and copies ran while one was open for 7% -> 5% of each run, Pallas kernels for 9% -> 10%
where the time goes in v5:
time: 164 us; the launch traced here: 163 us
  blocking collectives  66.3 us (40%)
  waiting for transfers between devices  29.5 us (18%)
  starting transfers between devices  19.7 us (12%)
  Pallas kernels  16.5 us (10%)
  between operations  16.4 us (10%)
  other arithmetic  7.89 us (5%)
  local copies, waits for them, and re-layouts  4.12 us (3%)
  matrix products  2.91 us (2%)
    all_to_all x4, blocking collectives, exchange(): return lax.all_to_all(x, axes, split_axis=0, concat_axis=0, tiled=True)  56.3 us
    ppermute x4, starting transfers between devices, swap(): return lax.ppermute(x, 'c', [(0, 1), (1, 0)])  15.5 us
    all_gather x1, waiting for transfers between devices, local(): feats_mine = lax.all_gather(feats_y, 'z', axis=0, tiled=True)  11.4 us
    all_gather x1, blocking collectives, local(): cot_rows = lax.all_gather(cotangent, 'x', axis=0, tiled=True)  9.96 us
    ppermute x4, waiting for transfers between devices, swap(): return lax.ppermute(x, 'c', [(0, 1), (1, 0)])  9.62 us
    pallas_call x1, Pallas kernels, forward(): pl.pallas_call(forward_kernel, in_specs=[SMEM] * 5 + [ANY] * 2 + [VMEM] *...  6.73 us
    all_to_all x1, waiting for transfers between devices, exchange(): return lax.all_to_all(x, axes, split_axis=0, concat_axis=0, tiled=True)  5.01 us
    pallas_call x1, Pallas kernels, backward(): pl.pallas_call(backward_kernel, in_specs=[SMEM] * 4 + [VMEM] * 3, out_spe...  4.94 us
  transfers between devices with their start and end apart: 8, of which 6 were waited for; matrix products, arithmetic and copies ran while one was open for 5% of the time, Pallas kernels for 10%

profile of v5, /device:TPU:1, one launch (start us, length us, event | category | flops | bytes accessed | tf_op | source)
XLA Modules:
  0.0 163.3 jit_solution(6057290146628881109)
XLA Ops:
  8.1 0.9 convert_reduce_fusion.2
  9.0 1.0 fusion
  10.0 10.4 %all_to_all.25 = bf16[4,128,256]{2,1,0:T(8,128)(2,1)} all-to-all(bf16[4,128,256]{2,1,0:T(8,128)(2,1)S(1)} %broadcast_in_dim.15), channel_id=1, replica_groups=mesh['y'=4,'z'=8,'c'=2,'x'=4] {'y'}, dimensions={0} | all-to-all | bytes 524288 | tf_op jit(solution)/shard_map/feats_y/all_to_all | solution.py:298
  21.2 0.7 pad.4
  21.9 0.7 add_add_fusion
  22.5 0.9 fusion.3.coef
  23.4 10.0 %all_gather.7.cot = bf16[512,256]{1,0:T(8,128)(2,1)S(1)} all-gather(bf16[128,256]{1,0:T(8,128)(2,1)} %param.19), channel_id=1, replica_groups=mesh['y'=4,'z'=8,'c'=2,'x'=4] {'x'}, dimensions={0}, use_global_device_ids=true | all-gather | bytes 327680 | tf_op jit(solution)/shard_map/cot_x/all_gather | solution.py:354
  33.4 4.9 %backward.1 = (bf16[4,8,128,256]{3,2,1,0:T(8,128)(2,1)}, bf16[32,128,256]{2,1,0:T(8,128)(2,1)S(1)}, bf16[32,128,256]{2,1,0:T(8,128)(2,1)S(1)}) custom-call(s32[32]{0:T(128)S(1)} %copy-done.3, s32[32]{0:T(128)S(1)} %get-tuple-element.46.dslot, s32[1]{0:T(128)S(6)} %copy.36.count, f32[40,8]{1,0:T(8,128)S(1)} %fusion.3.coef, ...), custom_call_target="tpu_custom_call" | custom-call | tf_op jit(solution)/shard_map/backward/pallas_call | solution.py:121
  38.4 4.9 %collective-permute-start.2 = (bf16[32,128,256]{2,1,0:T(8,128)(2,1)S(1)}, bf16[32,128,256]{2,1,0:T(8,128)(2,1)S(1)}, u32[]{:S(2)}, u32[]{:S(2)}) collective-permute-start(bf16[32,128,256]{2,1,0:T(8,128)(2,1)S(1)} %get-tuple-element.25), channel_id=1, source_target_pairs={{0,4},{4,0},{1,5},{5,1},{2,6},{6,2},{3,7},{7,3},{8,12},{12,8},{9,1... | collective-permute-start | bytes 6291464 | tf_op jit(solution)/shard_map/dx_c/ppermute | solution.py:294
  43.2 3.8 %collective-permute-done.2 = bf16[32,128,256]{2,1,0:T(8,128)(2,1)S(1)} collective-permute-done((bf16[32,128,256]{2,1,0:T(8,128)(2,1)S(1)}, bf16[32,128,256]{2,1,0:T(8,128)(2,1)S(1)}, u32[]{:S(2)}, u32[]{:S(2)}) %collective-permute-start.2) | collective-permute-done | bytes 2097184 | tf_op jit(solution)/shard_map/dx_c/ppermute | solution.py:294
  47.0 2.1 %add_convert_fusion = bf16[32,128,256]{2,1,0:T(8,128)(2,1)} fusion(bf16[32,128,256]{2,1,0:T(8,128)(2,1)S(1)} %collective-permute-done.2, bf16[32,128,256]{2,1,0:T(8,128)(2,1)S(1)} %get-tuple-element.24), kind=kLoop, calls=%fused_computation | loop fusion | flops 4194304 | bytes 6291456 | tf_op jit(solution)/shard_map/convert_element_type | solution.py:361
  49.1 11.4 %all-gather.2.cloned.1.call-done = bf16[4096,256]{1,0:T(8,128)(2,1)} async-done(((bf16[512,256]{1,0:T(8,128)(2,1)}), bf16[4096,256]{1,0:T(8,128)(2,1)}) %all-gather.2.cloned.1.call-update) | async-done | bytes 2097168 | tf_op jit(solution)/shard_map/feats_z/all_gather | solution.py:352
  60.5 4.5 %collective-permute-start = (bf16[32,128,256]{2,1,0:T(8,128)(2,1)}, bf16[32,128,256]{2,1,0:T(8,128)(2,1)S(1)}, u32[]{:S(2)}, u32[]{:S(2)}) collective-permute-start(bf16[32,128,256]{2,1,0:T(8,128)(2,1)} %bitcast.33), channel_id=1, source_target_pairs={{0,4},{4,0},{1,5},{5,1},{2,6},{6,2},{3,7},{7,3},{8,12},{12,8},{9,1... | collective-permute-start | bytes 6291464 | tf_op jit(solution)/shard_map/feats_c/ppermute | solution.py:294
  65.1 4.0 %collective-permute-done.xother = bf16[32,128,256]{2,1,0:T(8,128)(2,1)S(1)} collective-permute-done((bf16[32,128,256]{2,1,0:T(8,128)(2,1)}, bf16[32,128,256]{2,1,0:T(8,128)(2,1)S(1)}, u32[]{:S(2)}, u32[]{:S(2)}) %collective-permute-start) | collective-permute-done | bytes 2097184 | tf_op jit(solution)/shard_map/feats_c/ppermute | solution.py:294
  69.1 1.3 copy-done.4
  70.4 6.7 %forward.1 = (bf16[512,256]{1,0:T(8,128)(2,1)S(1)}, f32[1024,256]{1,0:T(8,128)S(1)}, bf16[1024,256]{1,0:T(8,128)(2,1)S(1)}, bf16[32,128,256]{2,1,0:T(8,128)(2,1)}) custom-call(s32[32]{0:T(128)S(1)} %copy-done.3, s32[32]{0:T(128)S(1)} %add_add_fusion.1.xslot, s32[1]{0:T(128)S(6)} %copy.36.count, s32[1]{0:T(128)} %bitcast.half, f32[40,8]{1,0:T(8,128)S(1)} %fusion.3.coef, ...), custom_call_target="tpu_custom_call" | custom-call | tf_op jit(solution)/shard_map/forward/pallas_call | solution.py:204
  77.1 0.2 collective-permute-start.1
  77.3 1.8 %collective-permute-done.1 = bf16[1024,256]{1,0:T(8,128)(2,1)S(1)} collective-permute-done((bf16[1024,256]{1,0:T(8,128)(2,1)S(1)}, bf16[1024,256]{1,0:T(8,128)(2,1)S(1)}, u32[]{:S(2)}, u32[]{:S(2)}) %collective-permute-start.1) | collective-permute-done | bytes 524320 | tf_op jit(solution)/shard_map/dv_c/ppermute | solution.py:294
  79.2 0.9 pad_maximum_fusion
  80.2 3.5 %reduce-scatter.3.cloned.1.call-done = bf16[1024,256]{1,0:T(8,128)(2,1)} async-done(((bf16[4096,256]{1,0:T(8,128)(2,1)}), bf16[1024,256]{1,0:T(8,128)(2,1)}) %reduce-scatter.3.cloned.1.call-update) | async-done | bytes 524304 | tf_op jit(solution)/shard_map/dx_y/reduce_scatter | solution.py:363
  83.7 4.1 %all-to-all-start.1 = ((bf16[4,384,256]{2,1,0:T(8,128)(2,1)}), bf16[4,384,256]{2,1,0:T(8,128)(2,1)S(1)}, u32[]{:S(2)}, u32[]{:S(2)}) async-start(bf16[4,384,256]{2,1,0:T(8,128)(2,1)} %pad_maximum_fusion), calls=%async_computation.2 | async-start | bytes 1572864 | tf_op jit(solution)/shard_map/dv_x/all_to_all | solution.py:298
  88.1 1.0 convert_element_type.85
  89.1 4.8 %gram.1 = f32[32,128]{1,0:T(8,128)S(1)} custom-call(s32[32]{0:T(128)S(1)} %copy-done.3, s32[1]{0:T(128)S(6)} %copy.36.count, s32[256,1]{1,0:T(8,128)S(1)} %broadcast_in_dim_reshape.8.relc, s32[1,256]{1,0:T(1,128)S(1)} %broadcast_in_dim_reshape.7.relr, bf16[32,128,256]{2,1,0:T(8,128)(2,1)} %get-tuple-element.29.sent, ...), custom_call_target="tpu_custom_call" | custom-call | tf_op jit(solution)/shard_map/gram/pallas_call | solution.py:275
  94.1 5.0 %all-to-all-done.1 = bf16[4,384,256]{2,1,0:T(8,128)(2,1)S(1)} async-done(((bf16[4,384,256]{2,1,0:T(8,128)(2,1)}), bf16[4,384,256]{2,1,0:T(8,128)(2,1)S(1)}, u32[]{:S(2)}, u32[]{:S(2)}) %all-to-all-start.1) | async-done | bytes 786464 | tf_op jit(solution)/shard_map/dv_x/all_to_all | solution.py:298
  99.3 19.3 %all_to_all.26 = bf16[32,16,256]{2,1,0:T(8,128)(2,1)S(1)} all-to-all(bf16[32,16,256]{2,1,0:T(8,128)(2,1)S(1)} %maximum_maximum_fusion.1), channel_id=1, replica_groups=mesh['y'=4,'z'=8,'c'=2,'x'=4] {'y','z'}, dimensions={0} | all-to-all | bytes 524288 | tf_op jit(solution)/shard_map/dv_yz/all_to_all | solution.py:298
  118.8 16.9 %all_to_all.27 = bf16[32,16,256]{2,1,0:T(8,128)(2,1)S(1)} all-to-all(bf16[32,16,256]{2,1,0:T(8,128)(2,1)S(1)} %broadcast_in_dim.19), channel_id=1, replica_groups=mesh['y'=4,'z'=8,'c'=2,'x'=4] {'y','z'}, dimensions={0} | all-to-all | bytes 524288 | tf_op jit(solution)/shard_map/all_yz/all_to_all | solution.py:298
  135.9 9.7 %all_to_all.28 = bf16[4,288,256]{2,1,0:T(8,128)(2,1)S(1)} all-to-all(bf16[4,288,256]{2,1,0:T(8,128)(2,1)S(1)} %broadcast_in_dim.20), channel_id=1, replica_groups=mesh['y'=4,'z'=8,'c'=2,'x'=4] {'x'}, dimensions={0} | all-to-all | bytes 1179648 | tf_op jit(solution)/shard_map/all_x/all_to_all | solution.py:298
  145.7 5.9 %collective-permute-start.3 = (bf16[1056,256]{1,0:T(8,128)(2,1)S(1)}, bf16[1056,256]{1,0:T(8,128)(2,1)S(1)}, u32[]{:S(2)}, u32[]{:S(2)}) collective-permute-start(bf16[1056,256]{1,0:T(8,128)(2,1)S(1)} %maximum_maximum_fusion), channel_id=1, source_target_pairs={{0,4},{4,0},{1,5},{5,1},{2,6},{6,2},{3,7},{7,3},{8,12},{12,8},{9,1... | collective-permute-start | bytes 1622024 | tf_op jit(solution)/shard_map/all_c/ppermute | solution.py:294
  151.6 0.6 slice.79
  152.3 1.0 fusion.1
  153.5 0.7 copy.34
  154.4 1.5 convert_multiply_fusion
  (60 shorter events, 1.6 us)
Async XLA Ops:
  8.0 1.0 copy-start
  8.0 25.4 %copy-start.2 = (bf16[8,256,256]{2,1,0:T(8,128)(2,1)S(1)}, bf16[8,256,256]{2,1,0:T(8,128)(2,1)}, u32[]{:S(2)}) copy-start(bf16[8,256,256]{2,1,0:T(8,128)(2,1)} %param.18) | copy-start | bytes 3145732
  8.0 25.4 %copy-start.1 = (bf16[32,128,128]{2,1,0:T(8,128)(2,1)S(1)}, bf16[32,128,128]{2,1,0:T(8,128)(2,1)}, u32[]{:S(2)}) copy-start(bf16[32,128,128]{2,1,0:T(8,128)(2,1)} %tiles.3) | copy-start | bytes 3145732
  8.0 25.4 %copy-start.3 = (s32[32]{0:T(128)S(1)}, s32[32]{0:T(128)}, u32[]{:S(2)}) copy-start(s32[32]{0:T(128)} %trow.5) | copy-start | bytes 388
  8.0 52.5 %all-gather.2.cloned.1.call-start = ((), (), s32[]{:S(2)}) async-start(), calls=%async_computation.7 | async-start | bytes 2359296 | tf_op jit(solution)/shard_map/feats_z/all_gather | solution.py:352
  20.5 63.1 %reduce-scatter.3.cloned.1.call-start = ((), (), s32[]{:S(2)}) async-start(), calls=%async_computation.8 | async-start | bytes 2621440 | tf_op jit(solution)/shard_map/dx_y/reduce_scatter | solution.py:363
  38.4 8.6 %collective-permute-start.2 = (bf16[32,128,256]{2,1,0:T(8,128)(2,1)S(1)}, bf16[32,128,256]{2,1,0:T(8,128)(2,1)S(1)}, u32[]{:S(2)}, u32[]{:S(2)}) collective-permute-start(bf16[32,128,256]{2,1,0:T(8,128)(2,1)S(1)} %get-tuple-element.25), channel_id=1, source_target_pairs={{0,4},{4,0},{1,5},{5,1},{2,6},{6,2},{3,7},{7,3},{8,12},{12,8},{9,1... | collective-permute-start | bytes 6291464 | tf_op jit(solution)/shard_map/dx_c/ppermute | solution.py:294
  60.5 8.5 %collective-permute-start = (bf16[32,128,256]{2,1,0:T(8,128)(2,1)}, bf16[32,128,256]{2,1,0:T(8,128)(2,1)S(1)}, u32[]{:S(2)}, u32[]{:S(2)}) collective-permute-start(bf16[32,128,256]{2,1,0:T(8,128)(2,1)} %bitcast.33), channel_id=1, source_target_pairs={{0,4},{4,0},{1,5},{5,1},{2,6},{6,2},{3,7},{7,3},{8,12},{12,8},{9,1... | collective-permute-start | bytes 6291464 | tf_op jit(solution)/shard_map/feats_c/ppermute | solution.py:294
  69.1 1.3 copy-start.4
  77.1 2.0 %collective-permute-start.1 = (bf16[1024,256]{1,0:T(8,128)(2,1)S(1)}, bf16[1024,256]{1,0:T(8,128)(2,1)S(1)}, u32[]{:S(2)}, u32[]{:S(2)}) collective-permute-start(bf16[1024,256]{1,0:T(8,128)(2,1)S(1)} %get-tuple-element.22), channel_id=1, source_target_pairs={{0,4},{4,0},{1,5},{5,1},{2,6},{6,2},{3,7},{7,3},{8,12},{12,8},{9,1... | collective-permute-start | bytes 1572872 | tf_op jit(solution)/shard_map/dv_c/ppermute | solution.py:294
  79.2 8.5 %copy-start.6 = (s32[32]{0:T(128)S(1)}, s32[32]{0:T(128)}, u32[]{:S(2)}) copy-start(s32[32]{0:T(128)} %param.15) | copy-start | bytes 388
  83.7 4.4 %copy-start.5 = (bf16[1024,256]{1,0:T(8,128)(2,1)S(1)}, bf16[1024,256]{1,0:T(8,128)(2,1)}, u32[]{:S(2)}) copy-start(bf16[1024,256]{1,0:T(8,128)(2,1)} %reduce-scatter.3.cloned.1.call-done) | copy-start | bytes 1572868
  83.7 15.4 %all-to-all-start.1 = ((bf16[4,384,256]{2,1,0:T(8,128)(2,1)}), bf16[4,384,256]{2,1,0:T(8,128)(2,1)S(1)}, u32[]{:S(2)}, u32[]{:S(2)}) async-start(bf16[4,384,256]{2,1,0:T(8,128)(2,1)} %pad_maximum_fusion), calls=%async_computation.2 | async-start | bytes 1572864 | tf_op jit(solution)/shard_map/dv_x/all_to_all | solution.py:298
  87.7 48.0 %reduce-scatter.5.cloned.1.call-start = ((), (), s32[]{:S(2)}) async-start(), calls=%async_computation.9 | async-start | bytes 1179648 | tf_op jit(solution)/shard_map/dx_z/reduce_scatter | solution.py:381
  135.8 16.4 %copy-start.7 = (f32[128,256]{1,0:T(8,128)S(1)}, f32[128,256]{1,0:T(8,128)}, u32[]{:S(2)}) copy-start(f32[128,256]{1,0:T(8,128)} %reduce-scatter.5.cloned.1.call-done) | copy-start | bytes 393220
  135.8 16.4 %copy-start.8 = (s32[256]{0:T(256)S(1)}, s32[256]{0:T(256)}, u32[]{:S(2)}) copy-start(s32[256]{0:T(256)} %param.11) | copy-start | bytes 3076
  145.7 7.6 %collective-permute-start.3 = (bf16[1056,256]{1,0:T(8,128)(2,1)S(1)}, bf16[1056,256]{1,0:T(8,128)(2,1)S(1)}, u32[]{:S(2)}, u32[]{:S(2)}) collective-permute-start(bf16[1056,256]{1,0:T(8,128)(2,1)S(1)} %maximum_maximum_fusion), channel_id=1, source_target_pairs={{0,4},{4,0},{1,5},{5,1},{2,6},{6,2},{3,7},{7,3},{8,12},{12,8},{9,1... | collective-permute-start | bytes 1622024 | tf_op jit(solution)/shard_map/all_c/ppermute | solution.py:294
Sparse Core Ops, SparseCore 0:
  20.6 39.8 all-gather.1
  94.2 37.9 reduce-scatter.4
Sparse Core Ops, SparseCore 1:
  49.2 34.4 reduce-scatter.2

commit v6 on v5

--- a/solution.py
+++ b/solution.py
@@ -203,7 +203,7 @@
 def forward(trow, xslot, count, half, coef, xmine, xother, tiles, stacked, cot_rows):
     return pl.pallas_call(
         forward_kernel,
-        in_specs=[SMEM] * 5 + [ANY] * 2 + [VMEM] * 3,
+        in_specs=[SMEM] * 5 + [ANY] + [VMEM] * 4,
         out_specs=[VMEM] * 3 + [ANY],
         out_shape=[
             pltpu.VMEM((TROWS * TILE, H), BF16),
@@ -225,7 +225,7 @@
         name="forward",
     )(
         trow, xslot, count, half, coef,
-        *map(far, (xmine, xother)), *map(near, (tiles, stacked, cot_rows)),
+        far(xmine), *map(near, (xother, tiles, stacked, cot_rows)),
     )
 
 
@@ -375,7 +375,6 @@
         dgot = swap(dgive)
     dv = (dkeep + dgot.astype(F32)).reshape(NX, 256, H).astype(BF16)
     send_x = jnp.concatenate([dv, outp.reshape(NX, TILE, H)], axis=1)
-    send_x, dx = after(send_x, dx)
     sent, dx = after(sent, dx.astype(F32))
     with jax.named_scope("dx_z"):
         dx = lax.psum_scatter(dx, "z", scatter_dimension=0, tiled=True)

time: 164 us -> 158 us (0.963)
  waiting for transfers between devices: 29.5 us -> 26.3 us
  Pallas kernels: 16.5 us -> 14.4 us
    reduce_scatter x1, waiting for transfers between devices: 3.47 us -> 0.28 us  [local(): dx = lax.psum_scatter(dx, 'y', scatter_dimension=0, tiled=True)]
  transfers between devices with their start and end apart: 8 -> 8, of which waited for: 6 -> 6; matrix products, arithmetic and copies ran while one was open for 5% -> 6% of each run, Pallas kernels for 10% -> 9%
where the time goes in v6:
time: 158 us; the launch traced here: 157 us
  blocking collectives  64.9 us (41%)
  waiting for transfers between devices  26.3 us (17%)
  starting transfers between devices  20.2 us (13%)
  between operations  16.4 us (10%)
  Pallas kernels  14.4 us (9%)
  other arithmetic  8.93 us (6%)
  matrix products  2.91 us (2%)
  local copies, waits for them, and re-layouts  2.8 us (2%)
    all_to_all x4, blocking collectives, exchange(): return lax.all_to_all(x, axes, split_axis=0, concat_axis=0, tiled=True)  54.9 us
    ppermute x4, starting transfers between devices, swap(): return lax.ppermute(x, 'c', [(0, 1), (1, 0)])  15.5 us
    all_gather x1, waiting for transfers between devices, local(): feats_mine = lax.all_gather(feats_y, 'z', axis=0, tiled=True)  11.8 us
    all_gather x1, blocking collectives, local(): cot_rows = lax.all_gather(cotangent, 'x', axis=0, tiled=True)  9.96 us
    ppermute x4, waiting for transfers between devices, swap(): return lax.ppermute(x, 'c', [(0, 1), (1, 0)])  9.57 us
    pallas_call x1, Pallas kernels, forward(): pl.pallas_call(forward_kernel, in_specs=[SMEM] * 5 + [ANY] + [VMEM] * 4,...  5.64 us
    all_to_all x1, starting transfers between devices, exchange(): return lax.all_to_all(x, axes, split_axis=0, concat_axis=0, tiled=True)  4.63 us
    all_to_all x1, waiting for transfers between devices, exchange(): return lax.all_to_all(x, axes, split_axis=0, concat_axis=0, tiled=True)  4.6 us
  transfers between devices with their start and end apart: 8, of which 6 were waited for; matrix products, arithmetic and copies ran while one was open for 6% of the time, Pallas kernels for 9%

profile of v6, /device:TPU:1, one launch (start us, length us, event | category | flops | bytes accessed | tf_op | source)
XLA Modules:
  0.0 156.8 jit_solution(5245023256669037064)
XLA Ops:
  8.1 0.9 convert_reduce_fusion.2
  9.0 1.0 fusion
  10.0 10.4 %all_to_all.25 = bf16[4,128,256]{2,1,0:T(8,128)(2,1)} all-to-all(bf16[4,128,256]{2,1,0:T(8,128)(2,1)S(1)} %broadcast_in_dim.15), channel_id=1, replica_groups=mesh['y'=4,'z'=8,'c'=2,'x'=4] {'y'}, dimensions={0} | all-to-all | bytes 524288 | tf_op jit(solution)/shard_map/feats_y/all_to_all | solution.py:298
  21.2 0.7 pad.4
  21.9 0.7 add_add_fusion
  22.5 0.9 fusion.3.coef
  23.4 10.0 %all_gather.7.cot = bf16[512,256]{1,0:T(8,128)(2,1)S(1)} all-gather(bf16[128,256]{1,0:T(8,128)(2,1)} %param.19), channel_id=1, replica_groups=mesh['y'=4,'z'=8,'c'=2,'x'=4] {'x'}, dimensions={0}, use_global_device_ids=true | all-gather | bytes 327680 | tf_op jit(solution)/shard_map/cot_x/all_gather | solution.py:354
  33.4 4.5 %backward.1 = (bf16[4,8,128,256]{3,2,1,0:T(8,128)(2,1)}, bf16[32,128,256]{2,1,0:T(8,128)(2,1)S(1)}, bf16[32,128,256]{2,1,0:T(8,128)(2,1)S(1)}) custom-call(s32[32]{0:T(128)S(1)} %copy-done.3, s32[32]{0:T(128)S(1)} %get-tuple-element.42.dslot, s32[1]{0:T(128)S(6)} %copy.36.count, f32[40,8]{1,0:T(8,128)S(1)} %fusion.3.coef, ...), custom_call_target="tpu_custom_call" | custom-call | tf_op jit(solution)/shard_map/backward/pallas_call | solution.py:121
  37.9 4.9 %collective-permute-start.2 = (bf16[32,128,256]{2,1,0:T(8,128)(2,1)S(1)}, bf16[32,128,256]{2,1,0:T(8,128)(2,1)S(1)}, u32[]{:S(2)}, u32[]{:S(2)}) collective-permute-start(bf16[32,128,256]{2,1,0:T(8,128)(2,1)S(1)} %get-tuple-element.24), channel_id=1, source_target_pairs={{0,4},{4,0},{1,5},{5,1},{2,6},{6,2},{3,7},{7,3},{8,12},{12,8},{9,1... | collective-permute-start | bytes 6291464 | tf_op jit(solution)/shard_map/dx_c/ppermute | solution.py:294
  42.8 3.8 %collective-permute-done.2 = bf16[32,128,256]{2,1,0:T(8,128)(2,1)S(1)} collective-permute-done((bf16[32,128,256]{2,1,0:T(8,128)(2,1)S(1)}, bf16[32,128,256]{2,1,0:T(8,128)(2,1)S(1)}, u32[]{:S(2)}, u32[]{:S(2)}) %collective-permute-start.2) | collective-permute-done | bytes 2097184 | tf_op jit(solution)/shard_map/dx_c/ppermute | solution.py:294
  46.6 2.1 %add_convert_fusion = bf16[32,128,256]{2,1,0:T(8,128)(2,1)} fusion(bf16[32,128,256]{2,1,0:T(8,128)(2,1)S(1)} %collective-permute-done.2, bf16[32,128,256]{2,1,0:T(8,128)(2,1)S(1)} %get-tuple-element.23), kind=kLoop, calls=%fused_computation | loop fusion | flops 4194304 | bytes 6291456 | tf_op jit(solution)/shard_map/convert_element_type | solution.py:361
  48.7 11.8 %all-gather.2.cloned.1.call-done = bf16[4096,256]{1,0:T(8,128)(2,1)} async-done(((bf16[512,256]{1,0:T(8,128)(2,1)}), bf16[4096,256]{1,0:T(8,128)(2,1)}) %all-gather.2.cloned.1.call-update) | async-done | bytes 2097168 | tf_op jit(solution)/shard_map/feats_z/all_gather | solution.py:352
  60.4 4.6 %collective-permute-start = (bf16[32,128,256]{2,1,0:T(8,128)(2,1)}, bf16[32,128,256]{2,1,0:T(8,128)(2,1)S(1)}, u32[]{:S(2)}, u32[]{:S(2)}) collective-permute-start(bf16[32,128,256]{2,1,0:T(8,128)(2,1)} %bitcast.33), channel_id=1, source_target_pairs={{0,4},{4,0},{1,5},{5,1},{2,6},{6,2},{3,7},{7,3},{8,12},{12,8},{9,1... | collective-permute-start | bytes 6291464 | tf_op jit(solution)/shard_map/feats_c/ppermute | solution.py:294
  65.1 4.0 %collective-permute-done.xother = bf16[32,128,256]{2,1,0:T(8,128)(2,1)S(1)} collective-permute-done((bf16[32,128,256]{2,1,0:T(8,128)(2,1)}, bf16[32,128,256]{2,1,0:T(8,128)(2,1)S(1)}, u32[]{:S(2)}, u32[]{:S(2)}) %collective-permute-start) | collective-permute-done | bytes 2097184 | tf_op jit(solution)/shard_map/feats_c/ppermute | solution.py:294
  69.1 5.6 %forward.1 = (bf16[512,256]{1,0:T(8,128)(2,1)S(1)}, f32[1024,256]{1,0:T(8,128)S(1)}, bf16[1024,256]{1,0:T(8,128)(2,1)S(1)}, bf16[32,128,256]{2,1,0:T(8,128)(2,1)}) custom-call(s32[32]{0:T(128)S(1)} %copy-done.3, s32[32]{0:T(128)S(1)} %add_add_fusion.1.xslot, s32[1]{0:T(128)S(6)} %copy.36.count, s32[1]{0:T(128)} %bitcast.half, f32[40,8]{1,0:T(8,128)S(1)} %fusion.3.coef, ...), custom_call_target="tpu_custom_call" | custom-call | tf_op jit(solution)/shard_map/forward/pallas_call | solution.py:204
  74.7 0.2 collective-permute-start.1
  74.9 1.8 %collective-permute-done.1 = bf16[1024,256]{1,0:T(8,128)(2,1)S(1)} collective-permute-done((bf16[1024,256]{1,0:T(8,128)(2,1)S(1)}, bf16[1024,256]{1,0:T(8,128)(2,1)S(1)}, u32[]{:S(2)}, u32[]{:S(2)}) %collective-permute-start.1) | collective-permute-done | bytes 524320 | tf_op jit(solution)/shard_map/dv_c/ppermute | solution.py:294
  76.8 0.9 pad_maximum_fusion
  77.8 4.6 %all-to-all-start.1 = ((bf16[4,384,256]{2,1,0:T(8,128)(2,1)}), bf16[4,384,256]{2,1,0:T(8,128)(2,1)S(1)}, u32[]{:S(2)}, u32[]{:S(2)}) async-start(bf16[4,384,256]{2,1,0:T(8,128)(2,1)} %pad_maximum_fusion), calls=%async_computation.1 | async-start | bytes 1572864 | tf_op jit(solution)/shard_map/dv_x/all_to_all | solution.py:298
  82.8 0.3 reduce-scatter.3.cloned.1.call-done
  83.0 2.1 %convert_element_type.85 = f32[1024,256]{1,0:T(8,128)} convert(bf16[1024,256]{1,0:T(8,128)(2,1)} %reduce-scatter.3.cloned.1.call-done) | non-fusion elementwise | flops 262144 | bytes 1572864 | tf_op jit(solution)/shard_map/convert_element_type | solution.py:378
  85.2 4.3 %gram.1 = f32[32,128]{1,0:T(8,128)S(1)} custom-call(s32[32]{0:T(128)S(1)} %copy-done.3, s32[1]{0:T(128)S(6)} %copy.36.count, s32[256,1]{1,0:T(8,128)S(1)} %broadcast_in_dim_reshape.8.relc, s32[1,256]{1,0:T(1,128)S(1)} %broadcast_in_dim_reshape.7.relr, bf16[32,128,256]{2,1,0:T(8,128)(2,1)} %get-tuple-element.25.sent, ...), custom_call_target="tpu_custom_call" | custom-call | tf_op jit(solution)/shard_map/gram/pallas_call | solution.py:275
  89.5 4.6 %all-to-all-done.1 = bf16[4,384,256]{2,1,0:T(8,128)(2,1)S(1)} async-done(((bf16[4,384,256]{2,1,0:T(8,128)(2,1)}), bf16[4,384,256]{2,1,0:T(8,128)(2,1)S(1)}, u32[]{:S(2)}, u32[]{:S(2)}) %all-to-all-start.1) | async-done | bytes 786464 | tf_op jit(solution)/shard_map/dv_x/all_to_all | solution.py:298
  94.4 19.0 %all_to_all.26 = bf16[32,16,256]{2,1,0:T(8,128)(2,1)S(1)} all-to-all(bf16[32,16,256]{2,1,0:T(8,128)(2,1)S(1)} %maximum_maximum_fusion.1), channel_id=1, replica_groups=mesh['y'=4,'z'=8,'c'=2,'x'=4] {'y','z'}, dimensions={0} | all-to-all | bytes 524288 | tf_op jit(solution)/shard_map/dv_yz/all_to_all | solution.py:298
  113.5 15.7 %all_to_all.27 = bf16[32,16,256]{2,1,0:T(8,128)(2,1)S(1)} all-to-all(bf16[32,16,256]{2,1,0:T(8,128)(2,1)S(1)} %broadcast_in_dim.19), channel_id=1, replica_groups=mesh['y'=4,'z'=8,'c'=2,'x'=4] {'y','z'}, dimensions={0} | all-to-all | bytes 524288 | tf_op jit(solution)/shard_map/all_yz/all_to_all | solution.py:298
  129.5 9.7 %all_to_all.28 = bf16[4,288,256]{2,1,0:T(8,128)(2,1)S(1)} all-to-all(bf16[4,288,256]{2,1,0:T(8,128)(2,1)S(1)} %broadcast_in_dim.20), channel_id=1, replica_groups=mesh['y'=4,'z'=8,'c'=2,'x'=4] {'x'}, dimensions={0} | all-to-all | bytes 1179648 | tf_op jit(solution)/shard_map/all_x/all_to_all | solution.py:298
  139.3 5.7 %collective-permute-start.3 = (bf16[1056,256]{1,0:T(8,128)(2,1)S(1)}, bf16[1056,256]{1,0:T(8,128)(2,1)S(1)}, u32[]{:S(2)}, u32[]{:S(2)}) collective-permute-start(bf16[1056,256]{1,0:T(8,128)(2,1)S(1)} %maximum_maximum_fusion), channel_id=1, source_target_pairs={{0,4},{4,0},{1,5},{5,1},{2,6},{6,2},{3,7},{7,3},{8,12},{12,8},{9,1... | collective-permute-start | bytes 1622024 | tf_op jit(solution)/shard_map/all_c/ppermute | solution.py:294
  145.1 0.6 slice.79
  145.7 1.0 fusion.1
  146.8 0.2 reshape.113
  147.0 0.7 copy.34
  147.8 1.5 convert_multiply_fusion
  (56 shorter events, 1.4 us)
Async XLA Ops:
  8.0 1.0 copy-start
  8.0 25.4 %copy-start.3 = (s32[32]{0:T(128)S(1)}, s32[32]{0:T(128)}, u32[]{:S(2)}) copy-start(s32[32]{0:T(128)} %trow.5) | copy-start | bytes 388
  8.0 25.4 %copy-start.1 = (bf16[32,128,128]{2,1,0:T(8,128)(2,1)S(1)}, bf16[32,128,128]{2,1,0:T(8,128)(2,1)}, u32[]{:S(2)}) copy-start(bf16[32,128,128]{2,1,0:T(8,128)(2,1)} %tiles.3) | copy-start | bytes 3145732
  8.0 25.4 %copy-start.2 = (bf16[8,256,256]{2,1,0:T(8,128)(2,1)S(1)}, bf16[8,256,256]{2,1,0:T(8,128)(2,1)}, u32[]{:S(2)}) copy-start(bf16[8,256,256]{2,1,0:T(8,128)(2,1)} %param.18) | copy-start | bytes 3145732
  8.0 52.4 %all-gather.2.cloned.1.call-start = ((), (), s32[]{:S(2)}) async-start(), calls=%async_computation.7 | async-start | bytes 2359296 | tf_op jit(solution)/shard_map/feats_z/all_gather | solution.py:352
  20.5 62.5 %reduce-scatter.3.cloned.1.call-start = ((), (), s32[]{:S(2)}) async-start(), calls=%async_computation.8 | async-start | bytes 2621440 | tf_op jit(solution)/shard_map/dx_y/reduce_scatter | solution.py:363
  37.9 8.7 %collective-permute-start.2 = (bf16[32,128,256]{2,1,0:T(8,128)(2,1)S(1)}, bf16[32,128,256]{2,1,0:T(8,128)(2,1)S(1)}, u32[]{:S(2)}, u32[]{:S(2)}) collective-permute-start(bf16[32,128,256]{2,1,0:T(8,128)(2,1)S(1)} %get-tuple-element.24), channel_id=1, source_target_pairs={{0,4},{4,0},{1,5},{5,1},{2,6},{6,2},{3,7},{7,3},{8,12},{12,8},{9,1... | collective-permute-start | bytes 6291464 | tf_op jit(solution)/shard_map/dx_c/ppermute | solution.py:294
  60.4 8.6 %collective-permute-start = (bf16[32,128,256]{2,1,0:T(8,128)(2,1)}, bf16[32,128,256]{2,1,0:T(8,128)(2,1)S(1)}, u32[]{:S(2)}, u32[]{:S(2)}) collective-permute-start(bf16[32,128,256]{2,1,0:T(8,128)(2,1)} %bitcast.33), channel_id=1, source_target_pairs={{0,4},{4,0},{1,5},{5,1},{2,6},{6,2},{3,7},{7,3},{8,12},{12,8},{9,1... | collective-permute-start | bytes 6291464 | tf_op jit(solution)/shard_map/feats_c/ppermute | solution.py:294
  74.7 2.0 %collective-permute-start.1 = (bf16[1024,256]{1,0:T(8,128)(2,1)S(1)}, bf16[1024,256]{1,0:T(8,128)(2,1)S(1)}, u32[]{:S(2)}, u32[]{:S(2)}) collective-permute-start(bf16[1024,256]{1,0:T(8,128)(2,1)S(1)} %get-tuple-element.20), channel_id=1, source_target_pairs={{0,4},{4,0},{1,5},{5,1},{2,6},{6,2},{3,7},{7,3},{8,12},{12,8},{9,1... | collective-permute-start | bytes 1572872 | tf_op jit(solution)/shard_map/dv_c/ppermute | solution.py:294
  76.8 5.6 %copy-start.4 = (s32[32]{0:T(128)S(1)}, s32[32]{0:T(128)}, u32[]{:S(2)}) copy-start(s32[32]{0:T(128)} %param.15) | copy-start | bytes 388
  77.8 16.3 %all-to-all-start.1 = ((bf16[4,384,256]{2,1,0:T(8,128)(2,1)}), bf16[4,384,256]{2,1,0:T(8,128)(2,1)S(1)}, u32[]{:S(2)}, u32[]{:S(2)}) async-start(bf16[4,384,256]{2,1,0:T(8,128)(2,1)} %pad_maximum_fusion), calls=%async_computation.1 | async-start | bytes 1572864 | tf_op jit(solution)/shard_map/dv_x/all_to_all | solution.py:298
  82.4 46.9 %reduce-scatter.5.cloned.1.call-start = ((), (), s32[]{:S(2)}) async-start(), calls=%async_computation.9 | async-start | bytes 1179648 | tf_op jit(solution)/shard_map/dx_z/reduce_scatter | solution.py:380
  129.4 16.3 %copy-start.5 = (f32[128,256]{1,0:T(8,128)S(1)}, f32[128,256]{1,0:T(8,128)}, u32[]{:S(2)}) copy-start(f32[128,256]{1,0:T(8,128)} %reduce-scatter.5.cloned.1.call-done) | copy-start | bytes 393220
  129.4 16.3 %copy-start.6 = (s32[256]{0:T(256)S(1)}, s32[256]{0:T(256)}, u32[]{:S(2)}) copy-start(s32[256]{0:T(256)} %param.11) | copy-start | bytes 3076
  139.3 7.4 %collective-permute-start.3 = (bf16[1056,256]{1,0:T(8,128)(2,1)S(1)}, bf16[1056,256]{1,0:T(8,128)(2,1)S(1)}, u32[]{:S(2)}, u32[]{:S(2)}) collective-permute-start(bf16[1056,256]{1,0:T(8,128)(2,1)S(1)} %maximum_maximum_fusion), channel_id=1, source_target_pairs={{0,4},{4,0},{1,5},{5,1},{2,6},{6,2},{3,7},{7,3},{8,12},{12,8},{9,1... | collective-permute-start | bytes 1622024 | tf_op jit(solution)/shard_map/all_c/ppermute | solution.py:294
Sparse Core Ops, SparseCore 0:
  20.6 39.7 all-gather.1
  85.9 36.7 reduce-scatter.4
Sparse Core Ops, SparseCore 1:
  48.8 34.2 reduce-scatter.2
